TPU v7x, 32 devices: a whole 2x2x4 slice. The times are simulated.
32 devices in a mesh: comp: 2 (over core), lat: 4 (over z), lon: 4 (over y, x).
Axes of the slice: x: 2, y: 2, z: 4, core: 2. Of those that a mesh axis runs over, the one named last changes fastest.
Arguments:
- increment: float32 [2, 8, 64, 2048], P('comp', None, 'lat', 'lon'), may hold values from -6 to 6
- diffusivity: float32 [2, 8, 64, 2048], P('comp', None, 'lat', 'lon'), may hold values from 0.03 to 0.24
- innovation: float32 [2, 8, 64, 2048], P('comp', None, 'lat', 'lon'), may hold values from -6 to 6
- land_mask: int32 [64, 2048], P('lat', 'lon'), may hold values 0 or 1
- pull_cells: int32 [2, 4, 4, 4, 8192], P('comp', 'lat', 'lon'), may hold values from 0 to 8191
- put_cells: int32 [2, 4, 4, 4, 8192], P('comp', 'lat', 'lon'), may hold values from 0 to 8191
- pull_weight: float32 [2, 4, 4, 4, 8192], P('comp', 'lat', 'lon'), may hold values from 0.2 to 0.8
- pull_count: int32 [2, 4, 4, 4], P('comp', 'lat', 'lon'), may hold values from 1 to 8192, 16384 in all within a row
Outputs:
- linear_state: float32 [2, 8, 64, 2048], P('comp', None, 'lat', 'lon')
- gradient: float32 [2, 8, 64, 2048], P('comp', None, 'lat', 'lon')
Inputs may be any that keep to these rules, and one draw needn't show every extreme that they name: `pull_count`: for each receiving block the counts over the 4 source bands add up to 16384, and the largest of them is 8192.
All inputs are finite; a program needn't handle non-finite values. No bound on the sum of `land_mask` on one device may be relied on, other than what follows from the above.
Results may differ from a plain program's by a relative error of at most 0.00002.
Values sent between devices are 32-bit elements; how exact they have to be, the bound alone decides.
A program may use at most 64 MiB of HBM per device.

v0:
```python
import jax
import jax.numpy as jnp
from jax import lax
from jax.sharding import PartitionSpec as P

NSTEP = 4


def partner_2(value, axis, stride):
    mask = 2**stride
    pairs = [(source, source ^ mask) for source in range(lax.axis_size(axis))]
    return lax.ppermute(value, axis, pairs)


def extended(cells, sides, width, closed):
    for axis, dim in sides:
        count = lax.axis_size(axis)
        ends = count if closed else count - 1
        head = lax.slice_in_dim(cells, 0, width, axis=dim)
        tail = lax.slice_in_dim(cells, cells.shape[dim] - width, cells.shape[dim], axis=dim)
        cells = jnp.concatenate(
            [
                lax.ppermute(tail, axis, [(i, (i + 1) % count) for i in range(ends)]),
                cells,
                lax.ppermute(head, axis, [((i + 1) % count, i) for i in range(ends)]),
            ],
            axis=dim,
        )
    return cells


def mirrored(rows):
    partner = rows
    for bit in range(lax.axis_size("lon").bit_length() - 1):
        partner = partner_2(partner, "lon", bit)
    return partner[:, :, :, ::-1]


def at_fold():
    return (lax.axis_index("comp") == 1) & (lax.axis_index("lat") == lax.axis_size("lat") - 1)


def neighbours(field):
    lat_padded = extended(field, (("lat", 2),), 1, False)
    lon_padded = extended(field, (("lon", 3),), 1, True)
    folded = mirrored(field[:, :, -1:, :])[:, :, 0, :]
    north_edge = jnp.where(at_fold(), folded, lat_padded[:, :, -1, :])
    north = jnp.concatenate([lat_padded[:, :, 2:-1, :], north_edge[:, :, None, :]], axis=2)
    east = lon_padded[:, :, :, 2:]
    west = lon_padded[:, :, :, :-2]
    south = lat_padded[:, :, :-2, :]
    return (east, west, south, north)


def advance(field, coefficients):
    east, west, south, north = neighbours(field)
    change = coefficients[0] * (east - field) + coefficients[1] * (west - field)
    change = change + coefficients[2] * (south - field)
    change = change + coefficients[3] * (north - field)
    return field + change


def local(
    increment, diffusivity, innovation, land_mask, pull_cells, put_cells, pull_weight, pull_count
):
    height = increment.shape[2]
    width = increment.shape[3]
    cells = height * width
    bands = lax.axis_size("lat")
    ocean = lax.axis_index("comp") == 1
    mask_plane = jnp.where(
        ocean, land_mask.astype(jnp.float32), jnp.ones_like(land_mask, jnp.float32)
    )
    mask_levels = mask_plane[None, None]
    stacked = jnp.concatenate([diffusivity, mask_levels], axis=1)
    near = neighbours(stacked)
    coefficients = [
        mask_levels * side[:, -1:] * 0.5 * (diffusivity + side[:, :-1]) for side in near
    ]

    def sweep(field):
        for step in range(NSTEP):
            field = advance(field, coefficients)
        return field

    pulled = pull_cells.reshape(bands, -1)
    placed = put_cells.reshape(bands, -1)
    slot_count = pulled.shape[1]
    live = jnp.arange(slot_count, dtype=jnp.int32)[None, :] < pull_count.reshape(bands, 1)
    live_weight = jnp.where(
        live, pull_weight.reshape(bands, -1), jnp.zeros((bands, slot_count), jnp.float32)
    )
    mask_flat = mask_plane.reshape(-1)
    state = sweep(increment)
    surface = mask_flat * state[0, 0].reshape(-1)
    other_surface = partner_2(surface[None, :], "comp", 0)
    chosen = pulled
    values = jnp.take_along_axis(
        lax.all_gather(other_surface, "lat", axis=0, tiled=True), chosen, axis=1
    )
    income = jax.ops.segment_sum(
        (live_weight * values).reshape(-1), placed.reshape(-1), num_segments=cells
    )
    linear_state = state.at[0, 0].add((mask_flat * income).reshape(height, width))
    residual = linear_state - innovation
    residual_surface = mask_flat * residual[0, 0].reshape(-1)
    outgoing = live_weight * jnp.take(residual_surface, placed)
    chosen = pulled
    segment_ids = chosen + (jnp.arange(1 * lax.axis_size("lat"), dtype=jnp.int32) * cells)[:, None]
    summed = jax.ops.segment_sum(
        outgoing.reshape(-1), segment_ids.reshape(-1), num_segments=1 * lax.axis_size("lat") * cells
    )
    band_sums = lax.psum_scatter(
        summed.reshape(1 * lax.axis_size("lat"), cells), "lat", scatter_dimension=0, tiled=True
    )
    returned = partner_2(band_sums, "comp", 0)[0]
    adjoint_state = residual.at[0, 0].add((mask_flat * returned).reshape(height, width))
    adjoint_state = sweep(adjoint_state)
    gradient = adjoint_state + increment
    return (linear_state, gradient)


def solution(mesh):
    placed = (
        P("comp", None, "lat", "lon"),
        P("comp", None, "lat", "lon"),
        P("comp", None, "lat", "lon"),
        P("lat", "lon"),
        P("comp", "lat", "lon", None, None),
        P("comp", "lat", "lon", None, None),
        P("comp", "lat", "lon", None, None),
        P("comp", "lat", "lon", None),
    )
    return jax.shard_map(
        local,
        mesh=mesh,
        in_specs=placed,
        out_specs=(P("comp", None, "lat", "lon"), P("comp", None, "lat", "lon")),
        check_vma=False,
    )
```

profile of v0, /device:TPU:0, one launch (start us, length us, event | category | flops | bytes accessed | tf_op | source)
XLA Modules:
  0.0 1010.0 jit_solution(3817903647271611282)
XLA Ops:
  9.0 3.0 collective-permute-start.6
  12.0 3.5 collective-permute-start.4
  16.2 3.5 collective-permute-start.5
  19.6 1.3 collective-permute-start.11
  21.2 1.6 collective-permute-start.10
  22.9 2.1 collective-permute-done.10
  25.0 1.3 collective-permute-start.8
  26.7 2.5 collective-permute-start
  29.7 3.9 collective-permute-done.7
  34.1 3.0 collective-permute-start.1
  37.1 1.7 collective-permute-done.2
  39.0 3.4 collective-permute-done.3
  43.3 1.3 collective-permute-start.17
  44.6 2.0 collective-permute-done.15
  47.2 4.9 collective-permute-start.14
  52.1 1.4 collective-permute-start.12
  54.6 1.8 collective-permute-done.12
  56.4 2.3 collective-permute-done.13
  59.1 1.3 collective-permute-start.23
  60.4 2.4 collective-permute-done.21
  63.5 3.9 collective-permute-start.20
  67.4 1.3 collective-permute-start.18
  69.9 1.8 collective-permute-done.18
  71.7 2.6 collective-permute-done.19
  75.4 1.3 collective-permute-start.29
  76.7 1.8 collective-permute-done.27
  79.2 3.6 collective-permute-start.26
  82.9 1.6 collective-permute-start.24
  85.4 1.8 collective-permute-done.24
  87.2 2.5 collective-permute-done.25
  91.4 14.2 %all-gather = f32[4,1,8192]{2,1,0:T(1,128)S(1)} all-gather(f32[1,1,8192]{2,1,0:T(1,128)S(1)} %bitcast.126), channel_id=1, replica_groups=mesh['comp'=2,'lat'=4,'lon'=4] {'lat'}, dimensions={0}, use_global_device_ids=true | all-gather | bytes 163840 | tf_op jit(solution)/shard_map/all_gather | solution.py:99
  105.6 275.7 %gather_fusion.1 = f32[32768]{0:T(1024)S(1)} fusion(f32[4,8192]{1,0:T(4,128)S(1)} %bitcast.88, s32[32768]{0:T(1024)S(1)} %bitcast.89), kind=kCustom, calls=%fused_computation.1 | custom fusion | bytes 524288 | tf_op jit(solution)/shard_map/jit(take_along_axis)/gather | solution.py:98
  381.4 171.1 %scatter_custom_fusion = f32[8192]{0:T(1024)S(1)} fusion(s32[32768]{0:T(1024)S(1)} %bitcast.94, f32[32768]{0:T(1024)S(1)} %select_multiply_fusion.1, f32[]{:T(128)} %constant.97.clone.1), kind=kCustom, calls=%fused_computation.200 | custom fusion | flops 32768 | bytes 32772 | tf_op jit(solution)/shard_map/scatter-add | solution.py:101
  553.2 180.5 %gather_fusion = f32[32768]{0:T(1024)S(1)} fusion(f32[8192]{0:T(1024)S(1)} %mul.238, s32[32768]{0:T(1024)S(1)} %broadcast_clamp_fusion), kind=kCustom, calls=%fused_computation | custom fusion | bytes 393216 | tf_op jit(solution)/shard_map/jit(_take)/gather | solution.py:107
  733.8 171.1 %scatter_custom_fusion.1 = f32[32768]{0:T(1024)S(1)} fusion(s32[32768]{0:T(1024)S(1)} %bitcast.105, f32[32768]{0:T(1024)S(1)} %select_multiply_fusion, f32[]{:T(128)} %constant.97.clone.1), kind=kCustom, calls=%fused_computation.166 | custom fusion | flops 32768 | bytes 131076 | tf_op jit(solution)/shard_map/scatter-add | solution.py:110
  906.3 31.0 %all-reduce.3.cloned.1.call-done = f32[4,8192]{1,0:T(4,128)} async-done(((f32[4,8192]{1,0:T(4,128)}), f32[4,8192]{1,0:T(4,128)}) %all-reduce.3.cloned.1.call-update) | async-done | bytes 131088
  937.4 1.6 constant_dynamic-slice_fusion
  939.1 1.2 collective-permute-done.31
  941.6 1.5 collective-permute-start.35
  943.1 1.3 collective-permute-start.37
  945.4 1.4 collective-permute-start.36
  946.9 3.6 collective-permute-start.34
  950.6 1.2 collective-permute-start.32
  953.1 1.8 collective-permute-done.32
  954.9 2.0 collective-permute-done.33
  957.3 1.3 collective-permute-start.43
  958.6 2.4 collective-permute-done.41
  961.0 1.5 collective-permute-start.42
  962.6 3.2 collective-permute-start.40
  968.3 2.0 collective-permute-done.38
  970.3 1.7 collective-permute-done.39
  972.5 1.3 collective-permute-start.49
  973.8 2.3 collective-permute-done.47
  976.1 1.6 collective-permute-start.48
  977.9 3.1 collective-permute-start.46
  981.9 1.1 collective-permute-start.45
  983.5 1.8 collective-permute-done.44
  985.3 1.8 collective-permute-done.45
  987.7 1.3 collective-permute-start.55
  989.0 2.4 collective-permute-done.53
  991.3 1.4 collective-permute-start.54
  992.8 3.2 collective-permute-start.52
  998.5 1.8 collective-permute-done.50
  1000.3 1.9 collective-permute-done.51
  (168 shorter events, 28.9 us)
Async XLA Ops:
  7.2 8.4 copy-start.1
  7.2 930.2 %all-reduce.3.cloned.1.call-start = ((), (), s32[]{:S(2)}) async-start(), calls=%async_computation | async-start | bytes 262144
  9.0 12.1 %copy-start = (f32[1,8,16,512]{3,2,1,0:T(8,128)S(1)}, f32[1,8,16,512]{3,2,1,0:T(8,128)}, u32[]{:S(2)}) copy-start(f32[1,8,16,512]{3,2,1,0:T(8,128)} %param.13) | copy-start | bytes 786436
  9.0 20.2 %collective-permute-start.6 = (f32[1,9,1,512]{3,2,1,0:T(1,128)S(1)}, f32[1,9,1,512]{3,2,1,0:T(1,128)S(1)}, u32[]{:S(2)}, u32[]{:S(2)}) collective-permute-start(f32[1,9,1,512]{3,2,1,0:T(1,128)S(1)} %get-tuple-element.37), channel_id=1, source_target_pairs={{0,1},{1,0},{2,3},{3,2},{4,5},{5,4},{6,7},{7,6},{8,9},{9,8},{10,11... | collective-permute-start | bytes 55304 | tf_op jit(solution)/shard_map/ppermute | solution.py:12
  12.0 26.8 %collective-permute-start.4 = (f32[1,9,1,512]{3,2,1,0:T(1,128)S(1)}, f32[1,9,1,512]{3,2,1,0:T(1,128)S(1)}, u32[]{:S(2)}, u32[]{:S(2)}) collective-permute-start(f32[1,9,1,512]{3,2,1,0:T(1,128)S(1)} %get-tuple-element.37), channel_id=1, source_target_pairs={{0,4},{4,8},{8,12},{1,5},{5,9},{9,13},{2,6},{6,10},{10,14},{3,7},{... | collective-permute-start | bytes 55304 | tf_op jit(solution)/shard_map/ppermute | solution.py:23
  15.6 5.6 collective-permute-start.9
  16.2 26.2 %collective-permute-start.5 = (f32[1,8,1,512]{3,2,1,0:T(1,128)S(1)}, f32[1,8,1,512]{3,2,1,0:T(1,128)S(1)}, u32[]{:S(2)}, u32[]{:S(2)}) collective-permute-start(f32[1,8,1,512]{3,2,1,0:T(1,128)S(1)} %get-tuple-element.67), channel_id=1, source_target_pairs={{0,4},{4,8},{8,12},{1,5},{5,9},{9,13},{2,6},{6,10},{10,14},{3,7},{... | collective-permute-start | bytes 49160 | tf_op jit(solution)/shard_map/ppermute | solution.py:23
  19.6 7.1 collective-permute-start.11
  21.2 3.8 collective-permute-start.10
  25.0 9.1 collective-permute-start.8
  26.7 10.3 %collective-permute-start = (f32[1,9,16,1]{3,2,1,0:T(8,128)S(1)}, f32[1,9,16,1]{3,2,1,0:T(8,128)S(1)}, u32[]{:S(2)}, u32[]{:S(2)}) collective-permute-start(f32[1,9,16,1]{3,2,1,0:T(8,128)S(1)} %get-tuple-element.35), channel_id=1, source_target_pairs={{1,0},{2,1},{3,2},{0,3},{5,4},{6,5},{7,6},{4,7},{9,8},{10,9},{11,1... | collective-permute-start | bytes 1736 | tf_op jit(solution)/shard_map/ppermute | solution.py:25
  29.2 4.4 collective-permute-start.7
  33.6 5.3 collective-permute-start.2
  34.1 4.9 collective-permute-start.1
  37.1 5.3 collective-permute-start.3
  42.3 0.9 copy-start.4
  42.8 3.8 collective-permute-start.15
  43.3 11.3 %collective-permute-start.17 = (f32[1,8,1,512]{3,2,1,0:T(1,128)S(1)}, f32[1,8,1,512]{3,2,1,0:T(1,128)S(1)}, u32[]{:S(2)}, u32[]{:S(2)}) collective-permute-start(f32[1,8,1,512]{3,2,1,0:T(1,128)S(1)} %get-tuple-element.62), channel_id=1, source_target_pairs={{4,0},{8,4},{12,8},{5,1},{9,5},{13,9},{6,2},{10,6},{14,10},{7,3},{... | collective-permute-start | bytes 49160 | tf_op jit(solution)/shard_map/ppermute | solution.py:25
  46.6 7.6 collective-permute-start.16
  47.2 11.5 %collective-permute-start.14 = (f32[1,8,1,512]{3,2,1,0:T(1,128)S(1)}, f32[1,8,1,512]{3,2,1,0:T(1,128)S(1)}, u32[]{:S(2)}, u32[]{:S(2)}) collective-permute-start(f32[1,8,1,512]{3,2,1,0:T(1,128)S(1)} %get-tuple-element.63), channel_id=1, source_target_pairs={{0,4},{4,8},{8,12},{1,5},{5,9},{9,13},{2,6},{6,10},{10,14},{3,7},{... | collective-permute-start | bytes 49160 | tf_op jit(solution)/shard_map/ppermute | solution.py:23
  52.1 4.3 collective-permute-start.12
  53.5 5.2 collective-permute-start.13
  59.0 3.8 collective-permute-start.21
  59.1 10.8 %collective-permute-start.23 = (f32[1,8,1,512]{3,2,1,0:T(1,128)S(1)}, f32[1,8,1,512]{3,2,1,0:T(1,128)S(1)}, u32[]{:S(2)}, u32[]{:S(2)}) collective-permute-start(f32[1,8,1,512]{3,2,1,0:T(1,128)S(1)} %get-tuple-element.58), channel_id=1, source_target_pairs={{4,0},{8,4},{12,8},{5,1},{9,5},{13,9},{6,2},{10,6},{14,10},{7,3},{... | collective-permute-start | bytes 49160 | tf_op jit(solution)/shard_map/ppermute | solution.py:25
  62.8 6.7 collective-permute-start.22
  63.5 10.8 %collective-permute-start.20 = (f32[1,8,1,512]{3,2,1,0:T(1,128)S(1)}, f32[1,8,1,512]{3,2,1,0:T(1,128)S(1)}, u32[]{:S(2)}, u32[]{:S(2)}) collective-permute-start(f32[1,8,1,512]{3,2,1,0:T(1,128)S(1)} %get-tuple-element.59), channel_id=1, source_target_pairs={{0,4},{4,8},{8,12},{1,5},{5,9},{9,13},{2,6},{6,10},{10,14},{3,7},{... | collective-permute-start | bytes 49160 | tf_op jit(solution)/shard_map/ppermute | solution.py:23
  67.4 4.3 collective-permute-start.18
  68.6 5.7 collective-permute-start.19
  74.6 3.8 collective-permute-start.27
  75.4 10.0 collective-permute-start.29
  78.4 6.5 collective-permute-start.28
  79.2 10.4 %collective-permute-start.26 = (f32[1,8,1,512]{3,2,1,0:T(1,128)S(1)}, f32[1,8,1,512]{3,2,1,0:T(1,128)S(1)}, u32[]{:S(2)}, u32[]{:S(2)}) collective-permute-start(f32[1,8,1,512]{3,2,1,0:T(1,128)S(1)} %get-tuple-element.55), channel_id=1, source_target_pairs={{0,4},{4,8},{8,12},{1,5},{5,9},{9,13},{2,6},{6,10},{10,14},{3,7},{... | collective-permute-start | bytes 49160 | tf_op jit(solution)/shard_map/ppermute | solution.py:23
  82.9 4.3 collective-permute-start.24
  84.5 5.2 collective-permute-start.25
  89.9 0.9 copy-start.6
  90.0 1.3 collective-permute-start.30
  381.3 171.2 %copy-start.5 = (f32[1,8,16,512]{3,2,1,0:T(8,128)S(1)}, f32[1,8,16,512]{3,2,1,0:T(8,128)}, u32[]{:S(2)}) copy-start(f32[1,8,16,512]{3,2,1,0:T(8,128)} %param.14) | copy-start | bytes 786436
  733.8 171.9 %copy-start.9 = (u32[32]{0:T(128)S(1)}, u32[32]{0:T(128)}, u32[]{:S(2)}) copy-start(u32[32]{0:T(128)} %constant.124) | copy-start | bytes 388
  904.9 36.6 %copy-start.7 = (s32[16,512]{1,0:T(8,128)S(1)}, s32[16,512]{1,0:T(8,128)}, u32[]{:S(2)}) copy-start(s32[16,512]{1,0:T(8,128)} %param.15) | copy-start | bytes 98308
  939.0 1.3 collective-permute-start.31
  941.6 3.8 collective-permute-start.35
  943.1 10.0 collective-permute-start.37
  945.4 7.3 collective-permute-start.36
  946.9 10.0 collective-permute-start.34
  950.6 4.3 collective-permute-start.32
  951.7 5.2 collective-permute-start.33
  957.2 3.8 collective-permute-start.41
  957.3 11.0 %collective-permute-start.43 = (f32[1,8,1,512]{3,2,1,0:T(1,128)S(1)}, f32[1,8,1,512]{3,2,1,0:T(1,128)S(1)}, u32[]{:S(2)}, u32[]{:S(2)}) collective-permute-start(f32[1,8,1,512]{3,2,1,0:T(1,128)S(1)} %get-tuple-element.46), channel_id=1, source_target_pairs={{4,0},{8,4},{12,8},{5,1},{9,5},{13,9},{6,2},{10,6},{14,10},{7,3},{... | collective-permute-start | bytes 49160 | tf_op jit(solution)/shard_map/ppermute | solution.py:25
  961.0 6.9 collective-permute-start.42
  962.6 9.4 collective-permute-start.40
  965.8 4.5 collective-permute-start.38
  966.8 5.2 collective-permute-start.39
  972.3 3.8 collective-permute-start.47
  972.5 11.0 %collective-permute-start.49 = (f32[1,8,1,512]{3,2,1,0:T(1,128)S(1)}, f32[1,8,1,512]{3,2,1,0:T(1,128)S(1)}, u32[]{:S(2)}, u32[]{:S(2)}) collective-permute-start(f32[1,8,1,512]{3,2,1,0:T(1,128)S(1)} %get-tuple-element.42), channel_id=1, source_target_pairs={{4,0},{8,4},{12,8},{5,1},{9,5},{13,9},{6,2},{10,6},{14,10},{7,3},{... | collective-permute-start | bytes 49160 | tf_op jit(solution)/shard_map/ppermute | solution.py:25
  976.1 6.9 collective-permute-start.48
  977.9 9.2 collective-permute-start.46
  981.0 4.3 collective-permute-start.44
  981.9 5.2 collective-permute-start.45
  987.4 3.9 collective-permute-start.53
  987.7 10.8 %collective-permute-start.55 = (f32[1,8,1,512]{3,2,1,0:T(1,128)S(1)}, f32[1,8,1,512]{3,2,1,0:T(1,128)S(1)}, u32[]{:S(2)}, u32[]{:S(2)}) collective-permute-start(f32[1,8,1,512]{3,2,1,0:T(1,128)S(1)} %get-tuple-element.38), channel_id=1, source_target_pairs={{4,0},{8,4},{12,8},{5,1},{9,5},{13,9},{6,2},{10,6},{14,10},{7,3},{... | collective-permute-start | bytes 49160 | tf_op jit(solution)/shard_map/ppermute | solution.py:25
  991.3 6.7 collective-permute-start.54
  992.8 9.4 collective-permute-start.52
  996.0 4.3 collective-permute-start.50
  997.0 5.2 collective-permute-start.51
  (3 other events, 2.3 us)
Sparse Core Ops, SparseCore 0:
  905.8 31.5 all-reduce.2
where the time goes:
time: 1010 us
  local copies, waits for them, and re-layouts  467 us (46%)
  other arithmetic  348 us (34%)
  waiting for transfers between devices  85.1 us (8%)
  starting transfers between devices  79.9 us (8%)
  between operations  15 us (1%)
  blocking collectives  14.2 us (1%)
    gather x1, local copies, waits for them, and re-layouts, local(): jnp.take_along_axis(lax.all_gather(other_surface, 'lat', axis=0, tiled=Tr...  276 us
    gather x1, local copies, waits for them, and re-layouts, local(): outgoing = live_weight * jnp.take(residual_surface, placed)  181 us
    scatter-add x1, other arithmetic, local(): jax.ops.segment_sum(outgoing.reshape(-1), segment_ids.reshape(-1), num_se...  171 us
    scatter-add x1, other arithmetic, local(): jax.ops.segment_sum((live_weight * values).reshape(-1), placed.reshape(-1...  171 us
    ppermute x18, starting transfers between devices, extended(): lax.ppermute(tail, axis, [(i, (i + 1) % count) for i in range(ends)])  38.5 us
    unnamed x2, waiting for transfers between devices  31.1 us
    ppermute x18, starting transfers between devices, extended(): lax.ppermute(head, axis, [((i + 1) % count, i) for i in range(ends)])  25.6 us
    ppermute x20, waiting for transfers between devices, partner_2(): return lax.ppermute(value, axis, pairs)  21.5 us
  transfers between devices with their start and end apart: 57, of which 27 were waited for; matrix products, arithmetic and copies ran while one was open for 1% of the time, Pallas kernels for 0%

commit v1 on v0

v1 whole, which is shorter than its diff:
```python
import functools

import jax
import jax.numpy as jnp
from jax import lax
from jax.experimental import pallas as pl
from jax.experimental.pallas import tpu as pltpu
from jax.sharding import PartitionSpec as P

NSTEP = 4
LANES = 128
HALO = 4


def shifted(value, amount, axis):
    return pltpu.roll(value, amount % value.shape[axis], axis)


def coefficients_of(diffusivity, mask):
    half = mask * 0.5
    pairs = ((-1, 1), (1, 1), (1, 0), (-1, 0))
    return [
        half * shifted(mask, by, axis) * (diffusivity + shifted(diffusivity, by, axis))
        for by, axis in pairs
    ]


def stepped(field, coefficients):
    east, west, south, north = coefficients
    change = east * (shifted(field, -1, 1) - field) + west * (shifted(field, 1, 1) - field)
    change = change + south * (shifted(field, 1, 0) - field)
    change = change + north * (shifted(field, -1, 0) - field)
    return field + change


def forward_kernel(height, width, field_ref, extended_ref, state_ref):
    levels = field_ref.shape[0]
    mask = extended_ref[levels]

    def level(at, carry):
        coefficients = coefficients_of(extended_ref[at], mask)
        field = field_ref[at]
        for _ in range(NSTEP):
            field = stepped(field, coefficients)
        state_ref[at] = field[:height, :width]
        return carry

    lax.fori_loop(0, levels, level, 0)


def adjoint_kernel(height, width, field_ref, extended_ref, increment_ref, gradient_ref):
    levels = field_ref.shape[0]
    mask = extended_ref[levels]

    def level(at, carry):
        coefficients = coefficients_of(extended_ref[at], mask)
        field = field_ref[at]
        for _ in range(NSTEP):
            field = stepped(field, coefficients)
        gradient_ref[at] = field[:height, :width] + increment_ref[at]
        return carry

    lax.fori_loop(0, levels, level, 0)


def table_of(plane):
    parts = [plane[:, at : at + LANES] for at in range(0, plane.shape[1], LANES)]
    return jnp.concatenate(parts, axis=0)


def plane_of(table, height):
    parts = [table[at : at + height] for at in range(0, table.shape[0], height)]
    return jnp.concatenate(parts, axis=1)


def split_cell(cell, height, width):
    row = cell // width
    column = cell - row * width
    tile = column // LANES
    return tile * height + row, column - tile * LANES


def looked_up(table_ref, index, high, low):
    rows = table_ref.shape[-2]

    def one(row, found):
        line = jnp.broadcast_to(table_ref[index + (pl.ds(row, 1), slice(None))], low.shape)
        return jnp.where(high == row, jnp.take_along_axis(line, low, axis=1), found)

    found = jnp.zeros(low.shape, jnp.float32)
    for row in range(rows):
        found = one(row, found)
    return found


def spread(values, high, low, rows):
    first = values.astype(jnp.bfloat16).astype(jnp.float32)
    second = values - first
    row_at = lax.broadcasted_iota(jnp.int32, (rows, LANES), 0)
    lane_at = lax.broadcasted_iota(jnp.int32, (LANES, LANES), 0)
    left, right = [], []
    for r in range(values.shape[0]):
        hit = high[r : r + 1] == row_at
        top = jnp.where(hit, first[r : r + 1], 0.0).astype(jnp.bfloat16)
        bottom = jnp.where(hit, second[r : r + 1], 0.0).astype(jnp.bfloat16)
        left.append(jnp.concatenate([top, bottom], axis=0))
        right.append(jnp.where(low[r : r + 1] == lane_at, 1.0, 0.0).astype(jnp.bfloat16))
    return lax.dot_general(
        jnp.concatenate(left, axis=1),
        jnp.concatenate(right, axis=1),
        (((1,), (1,)), ((), ())),
        preferred_element_type=jnp.float32,
    )


def couple_kernel(
    height,
    width,
    count_ref,
    source_ref,
    pull_ref,
    put_ref,
    weight_ref,
    mask_ref,
    state_ref,
    innovation_ref,
    linear_ref,
    adjoint_ref,
    sums_ref,
    total_ref,
    residual_ref,
):
    bands = source_ref.shape[0]
    lines = pull_ref.shape[1]
    rows = height * width // LANES
    deep = min(8, lines)
    block = deep * LANES
    slot = lax.broadcasted_iota(jnp.int32, (deep, LANES), 0) * LANES
    slot = slot + lax.broadcasted_iota(jnp.int32, (deep, LANES), 1)

    def slots(band, at):
        where = pl.ds(pl.multiple_of(at * deep, deep), deep)
        pull = split_cell(pull_ref[band, where, :], height, width)
        put = split_cell(put_ref[band, where, :], height, width)
        live = slot + at * block < count_ref[band]
        return pull, put, jnp.where(live, weight_ref[band, where, :], 0.0)

    def blocks(band):
        return (count_ref[band] + block - 1) // block

    total_ref[...] = jnp.zeros_like(total_ref)

    def forward_band(band, carry):
        def body(at, carry):
            pull, put, weight = slots(band, at)
            values = weight * looked_up(source_ref, (band,), *pull)
            total_ref[...] += spread(values, *put, rows)
            return carry

        return lax.fori_loop(0, blocks(band), body, carry)

    lax.fori_loop(0, bands, forward_band, 0)
    mask = mask_ref[...]
    income = plane_of(total_ref[:rows] + total_ref[rows:], height)
    linear_ref[...] = state_ref[...]
    linear_ref[0] = state_ref[0] + mask * income
    adjoint_ref[...] = linear_ref[...] - innovation_ref[...]
    residual_ref[...] = table_of(mask * adjoint_ref[0])

    def backward_band(band, carry):
        total_ref[...] = jnp.zeros_like(total_ref)

        def body(at, carry):
            pull, put, weight = slots(band, at)
            values = weight * looked_up(residual_ref, (), *put)
            total_ref[...] += spread(values, *pull, rows)
            return carry

        lax.fori_loop(0, blocks(band), body, 0)
        sums_ref[band] = total_ref[:rows] + total_ref[rows:]
        return carry

    lax.fori_loop(0, bands, backward_band, 0)


def over(axis, value, pairs):
    return lax.ppermute(value, axis, pairs)


def extended(cells):
    lons = lax.axis_size("lon")
    lats = lax.axis_size("lat")
    height, width = cells.shape[1:]
    round_up = [(i, (i + 1) % lons) for i in range(lons)]
    round_down = [((i + 1) % lons, i) for i in range(lons)]
    west = over("lon", cells[:, :, width - HALO :], round_up)
    east = over("lon", cells[:, :, :HALO], round_down)
    gap = jnp.zeros(cells.shape[:2] + (LANES - 2 * HALO,), cells.dtype)
    wide = jnp.concatenate([cells, east, gap, west], axis=2)
    up = [(i, i + 1) for i in range(lats - 1)]
    down = [(i + 1, i) for i in range(lats - 1)]
    south = over("lat", wide[:, height - HALO :], up)
    north = over("lat", wide[:, :HALO], down)
    mirror = over("lon", wide[:, height - HALO :], [(i, lons - 1 - i) for i in range(lons)])
    mirror = jnp.roll(mirror[:, ::-1, ::-1], -LANES, axis=2)
    fold = (lax.axis_index("comp") == 1) & (lax.axis_index("lat") == lats - 1)
    return jnp.concatenate([wide, jnp.where(fold, mirror, north), south], axis=1)


def local(
    increment, diffusivity, innovation, land_mask, pull_cells, put_cells, pull_weight, pull_count
):
    levels, height, width = increment.shape[1:]
    bands = lax.axis_size("lat")
    rows = height * width // LANES
    capacity = pull_cells.shape[-1]
    lines = capacity // LANES
    ocean = lax.axis_index("comp") == 1
    mask = jnp.where(ocean, land_mask.astype(jnp.float32), jnp.ones(land_mask.shape, jnp.float32))
    whole = pl.BlockSpec(memory_space=pltpu.VMEM)
    params = pltpu.CompilerParams(vmem_limit_bytes=48 * 1024 * 1024)
    block = jax.ShapeDtypeStruct((levels, height, width), jnp.float32)

    fixed = jnp.concatenate([diffusivity[0], mask[None]], axis=0)
    both = extended(jnp.concatenate([increment[0], fixed], axis=0))
    state = pl.pallas_call(
        functools.partial(forward_kernel, height, width),
        out_shape=block,
        in_specs=[whole, whole],
        out_specs=whole,
        compiler_params=params,
    )(both[:levels], both[levels:])

    surface = table_of(mask * state[0])
    swap = [(0, 1), (1, 0)]
    source = lax.all_gather(over("comp", surface, swap), "lat", axis=0, tiled=False)
    linear, adjoint, sums = pl.pallas_call(
        functools.partial(couple_kernel, height, width),
        out_shape=(block, block, jax.ShapeDtypeStruct((bands, rows, LANES), jnp.float32)),
        in_specs=[pl.BlockSpec(memory_space=pltpu.SMEM)] + [whole] * 7,
        out_specs=(whole, whole, whole),
        scratch_shapes=[
            pltpu.VMEM((2 * rows, LANES), jnp.float32),
            pltpu.VMEM((rows, LANES), jnp.float32),
        ],
        compiler_params=params,
    )(
        pull_count.reshape(bands),
        source,
        pull_cells.reshape(bands, lines, LANES),
        put_cells.reshape(bands, lines, LANES),
        pull_weight.reshape(bands, lines, LANES),
        mask,
        state,
        innovation[0],
    )
    band_sums = lax.psum_scatter(sums, "lat", scatter_dimension=0, tiled=False)
    returned = plane_of(over("comp", band_sums, swap), height)
    adjoint = adjoint.at[0].add(mask * returned)
    gradient = pl.pallas_call(
        functools.partial(adjoint_kernel, height, width),
        out_shape=block,
        in_specs=[whole, whole, whole],
        out_specs=whole,
        compiler_params=params,
    )(extended(adjoint), both[levels:], increment[0])
    return (linear[None], gradient[None])


def solution(mesh):
    placed = (
        P("comp", None, "lat", "lon"),
        P("comp", None, "lat", "lon"),
        P("comp", None, "lat", "lon"),
        P("lat", "lon"),
        P("comp", "lat", "lon", None, None),
        P("comp", "lat", "lon", None, None),
        P("comp", "lat", "lon", None, None),
        P("comp", "lat", "lon", None),
    )
    return jax.shard_map(
        local,
        mesh=mesh,
        in_specs=placed,
        out_specs=(P("comp", None, "lat", "lon"), P("comp", None, "lat", "lon")),
        check_vma=False,
    )
```

time: 1010 us -> 114 us (0.11)
  local copies, waits for them, and re-layouts: 467 us -> 3.05 us
  other arithmetic: 348 us -> 2.54 us
  starting transfers between devices: 79.9 us -> 20.2 us
  waiting for transfers between devices: 85.1 us -> 37.5 us
  Pallas kernels: 0 us -> 22 us
    gather x2 -> x0, local copies, waits for them, and re-layouts: 456 us -> none  [the longest x1 276 us: local(): jnp.take_along_axis(lax.all_gather(other_surface, 'lat', axis=0, tiled=Tr...]
    scatter-add x4 -> x1, other arithmetic: 342 us -> 0.01 us  [local(): adjoint = adjoint.at[0].add(mask * returned)]
    ppermute x56 -> x12, starting transfers between devices: 79.8 us -> 20.2 us  [over(): return lax.ppermute(value, axis, pairs)]
    ppermute x56 -> x12, waiting for transfers between devices: 54.1 us -> 17.3 us  [over(): return lax.ppermute(value, axis, pairs)]
    unnamed x2 -> x1, waiting for transfers between devices: 31.1 us -> 0.02 us
    pallas_call x0 -> x3, Pallas kernels: none -> 22 us  [the longest x1 14.1 us: local(): pl.pallas_call(functools.partial(couple_kernel, height, width), out_shape...]
    reduce_scatter x0 -> x1, waiting for transfers between devices: none -> 20.2 us  [local(): band_sums = lax.psum_scatter(sums, 'lat', scatter_dimension=0, tiled=False)]
  transfers between devices with their start and end apart: 57 -> 13, of which waited for: 27 -> 10; matrix products, arithmetic and copies ran while one was open for 1% -> 1% of each run, Pallas kernels for 0% -> 0%
where the time goes in v1:
time: 114 us
  waiting for transfers between devices  37.5 us (33%)
  Pallas kernels  22 us (19%)
  starting transfers between devices  20.2 us (18%)
  blocking collectives  14.5 us (13%)
  between operations  14.4 us (13%)
  local copies, waits for them, and re-layouts  3.05 us (3%)
  other arithmetic  2.54 us (2%)
    reduce_scatter x1, waiting for transfers between devices, local(): band_sums = lax.psum_scatter(sums, 'lat', scatter_dimension=0, tiled=False)  20.2 us
    ppermute x12, starting transfers between devices, over(): return lax.ppermute(value, axis, pairs)  20.2 us
    ppermute x12, waiting for transfers between devices, over(): return lax.ppermute(value, axis, pairs)  17.3 us
    all_gather x1, blocking collectives, local(): lax.all_gather(over('comp', surface, swap), 'lat', axis=0, tiled=False)  14.5 us
    pallas_call x1, Pallas kernels, local(): pl.pallas_call(functools.partial(couple_kernel, height, width), out_shape...  14.1 us
    pallas_call x1, Pallas kernels, local(): pl.pallas_call(functools.partial(adjoint_kernel, height, width), out_shap...  4.28 us
    pallas_call x1, Pallas kernels, local(): pl.pallas_call(functools.partial(forward_kernel, height, width), out_shap...  3.56 us
  transfers between devices with their start and end apart: 13, of which 10 were waited for; matrix products, arithmetic and copies ran while one was open for 1% of the time, Pallas kernels for 0%

profile of v1, /device:TPU:0, one launch (start us, length us, event | category | flops | bytes accessed | tf_op | source)
XLA Modules:
  0.0 114.1 jit_solution(15445132539379803362)
XLA Ops:
  7.2 0.0 reduce-scatter.2.cloned.1.call-start
  7.2 0.8 fusion.7
  8.0 0.0 copy-start
  8.0 0.0 copy-start.3
  8.0 1.1 pad_maximum_fusion.10
  9.1 3.9 %collective-permute-start = (f32[17,16,4]{2,1,0:T(8,128)S(1)}, f32[17,16,4]{2,1,0:T(8,128)S(1)}, u32[]{:S(2)}, u32[]{:S(2)}) collective-permute-start(f32[17,16,4]{2,1,0:T(8,128)S(1)} %get-tuple-element.22), channel_id=1, source_target_pairs={{1,0},{2,1},{3,2},{0,3},{5,4},{6,5},{7,6},{4,7},{9,8},{10,9},{11,1... | collective-permute-start | bytes 13064 | tf_op jit(solution)/shard_map/ppermute | solution.py:187
  13.0 0.0 collective-permute-start.1
  13.0 4.1 %collective-permute-done = f32[17,16,4]{2,1,0:T(8,128)S(1)} collective-permute-done((f32[17,16,4]{2,1,0:T(8,128)S(1)}, f32[17,16,4]{2,1,0:T(8,128)S(1)}, u32[]{:S(2)}, u32[]{:S(2)}) %collective-permute-start) | collective-permute-done | bytes 4384 | tf_op jit(solution)/shard_map/ppermute | solution.py:187
  17.1 2.8 %collective-permute-done.1 = f32[17,16,4]{2,1,0:T(8,128)S(1)} collective-permute-done((f32[17,16,4]{2,1,0:T(8,128)S(1)}, f32[17,16,4]{2,1,0:T(8,128)S(1)}, u32[]{:S(2)}, u32[]{:S(2)}) %collective-permute-start.1) | collective-permute-done | bytes 4384 | tf_op jit(solution)/shard_map/ppermute | solution.py:187
  19.9 0.0 copy-done
  20.0 0.0 copy-done.3
  20.0 0.0 copy-start.6
  20.0 0.0 copy-start.7
  20.0 0.2 pad_maximum_fusion.2
  20.2 1.5 %collective-permute-start.2 = (f32[17,4,640]{2,1,0:T(4,128)S(1)}, f32[17,4,640]{2,1,0:T(4,128)S(1)}, u32[]{:S(2)}, u32[]{:S(2)}) collective-permute-start(f32[17,4,640]{2,1,0:T(4,128)S(1)} %get-tuple-element.21), channel_id=1, source_target_pairs={{0,3},{1,2},{2,1},{3,0},{4,7},{5,6},{6,5},{7,4},{8,11},{9,10},{10,... | collective-permute-start | bytes 522248 | tf_op jit(solution)/shard_map/ppermute | solution.py:187
  21.7 1.3 %collective-permute-start.3 = (f32[17,4,640]{2,1,0:T(4,128)S(1)}, f32[17,4,640]{2,1,0:T(4,128)S(1)}, u32[]{:S(2)}, u32[]{:S(2)}) collective-permute-start(f32[17,4,640]{2,1,0:T(4,128)S(1)} %get-tuple-element.20), channel_id=1, source_target_pairs={{4,0},{8,4},{12,8},{5,1},{9,5},{13,9},{6,2},{10,6},{14,10},{7,3},{... | collective-permute-start | bytes 522248 | tf_op jit(solution)/shard_map/ppermute | solution.py:187
  23.0 0.0 copy-done.6
  23.0 0.0 copy-done.7
  23.0 4.6 %collective-permute-start.4 = (f32[17,4,640]{2,1,0:T(4,128)S(1)}, f32[17,4,640]{2,1,0:T(4,128)S(1)}, u32[]{:S(2)}, u32[]{:S(2)}) collective-permute-start(f32[17,4,640]{2,1,0:T(4,128)S(1)} %get-tuple-element.21), channel_id=1, source_target_pairs={{0,4},{4,8},{8,12},{1,5},{5,9},{9,13},{2,6},{6,10},{10,14},{3,7},{... | collective-permute-start | bytes 522248 | tf_op jit(solution)/shard_map/ppermute | solution.py:187
  27.6 0.0 collective-permute-done.2
  27.6 0.6 slice.114
  28.2 0.1 slice.116
  28.4 0.6 collective-permute-done.3
  29.0 0.1 maximum_select_fusion
  29.0 1.4 %collective-permute-done.4 = f32[17,4,640]{2,1,0:T(4,128)S(1)} collective-permute-done((f32[17,4,640]{2,1,0:T(4,128)S(1)}, f32[17,4,640]{2,1,0:T(4,128)S(1)}, u32[]{:S(2)}, u32[]{:S(2)}) %collective-permute-start.4) | collective-permute-done | bytes 174112 | tf_op jit(solution)/shard_map/ppermute | solution.py:187
  30.5 0.2 pad_maximum_fusion
  30.8 0.0 copy-start.4
  30.8 3.6 %shard_map.95.state_ref = f32[8,16,512]{2,1,0:T(8,128)S(1)} custom-call(f32[8,24,640]{2,1,0:T(8,128)S(1)} %slice.140.field_ref, f32[9,24,640]{2,1,0:T(8,128)S(1)} %slice.141.extended_ref), custom_call_target="tpu_custom_call" | custom-call | tf_op jit(solution)/shard_map/pallas_call | solution.py:226
  34.3 0.0 copy-done.4
  34.4 0.0 copy-start.5
  34.4 0.0 copy-start.1
  34.4 0.1 collective-permute-start.5
  34.5 0.7 copy-done.5
  35.3 0.4 collective-permute-done.5
  35.7 14.5 %all-gather = f32[256,128]{1,0:T(8,128)S(1)} all-gather(f32[64,128]{1,0:T(8,128)S(1)} %collective-permute-done.5), channel_id=2, replica_groups=mesh['comp'=2,'lat'=4,'lon'=4] {'lat'}, dimensions={0}, use_global_device_ids=true | all-gather | bytes 163840 | tf_op jit(solution)/shard_map/all_gather | solution.py:236
  50.2 0.0 copy-start.2
  50.2 0.0 copy-done.1
  50.2 0.7 copy-done.2
  50.8 14.1 %shard_map.96 = (f32[8,16,512]{2,1,0:T(8,128)}, f32[8,16,512]{2,1,0:T(8,128)S(1)}, f32[4,64,128]{2,1,0:T(8,128)}) custom-call(s32[4]{0:T(128)S(1)} %bitcast.40, f32[4,64,128]{2,1,0:T(8,128)S(1)} %bitcast.37, s32[4,64,128]{2,1,0:T(8,128)S(1)} %get-tuple-element.37.pull_ref, s32[4,64,128]{2,1,0:T(8,128)S(1)} %get-tuple-element.36.put_ref, ...), custom_call_target="tpu_custom_call" | custom-call | tf_op jit(solution)/shard_map/pallas_call | solution.py:237
  65.0 0.0 reduce-scatter.2.cloned.1.call-update
  65.0 20.2 %reduce-scatter.2.cloned.1.call-done = f32[1,64,128]{2,1,0:T(8,128)} async-done(((f32[4,64,128]{2,1,0:T(8,128)}), f32[1,64,128]{2,1,0:T(8,128)}) %reduce-scatter.2.cloned.1.call-update) | async-done | bytes 32784 | tf_op jit(solution)/shard_map/reduce_scatter | solution.py:257
  85.2 0.0 collective-permute-start.6
  85.2 1.4 %collective-permute-done.6 = f32[64,128]{1,0:T(8,128)S(1)} collective-permute-done((f32[64,128]{1,0:T(8,128)}, f32[64,128]{1,0:T(8,128)S(1)}, u32[]{:S(2)}, u32[]{:S(2)}) %collective-permute-start.6) | collective-permute-done | bytes 32800 | tf_op jit(solution)/shard_map/ppermute | solution.py:187
  86.6 0.1 fusion.4
  86.7 2.3 %collective-permute-start.7 = (f32[8,16,4]{2,1,0:T(8,128)S(1)}, f32[8,16,4]{2,1,0:T(8,128)S(1)}, u32[]{:S(2)}, u32[]{:S(2)}) collective-permute-start(f32[8,16,4]{2,1,0:T(8,128)S(1)} %get-tuple-element.26), channel_id=1, source_target_pairs={{1,0},{2,1},{3,2},{0,3},{5,4},{6,5},{7,6},{4,7},{9,8},{10,9},{11,1... | collective-permute-start | bytes 6152 | tf_op jit(solution)/shard_map/ppermute | solution.py:187
  89.0 0.0 collective-permute-start.8
  89.1 2.4 %collective-permute-done.7 = f32[8,16,4]{2,1,0:T(8,128)S(1)} collective-permute-done((f32[8,16,4]{2,1,0:T(8,128)S(1)}, f32[8,16,4]{2,1,0:T(8,128)S(1)}, u32[]{:S(2)}, u32[]{:S(2)}) %collective-permute-start.7) | collective-permute-done | bytes 2080 | tf_op jit(solution)/shard_map/ppermute | solution.py:187
  91.4 2.8 %collective-permute-done.8 = f32[8,16,4]{2,1,0:T(8,128)S(1)} collective-permute-done((f32[8,16,4]{2,1,0:T(8,128)S(1)}, f32[8,16,4]{2,1,0:T(8,128)S(1)}, u32[]{:S(2)}, u32[]{:S(2)}) %collective-permute-start.8) | collective-permute-done | bytes 2080 | tf_op jit(solution)/shard_map/ppermute | solution.py:187
  94.2 0.1 pad_maximum_fusion.11
  94.3 0.7 collective-permute-start.9
  95.0 1.3 %collective-permute-start.10 = (f32[8,4,640]{2,1,0:T(4,128)S(1)}, f32[8,4,640]{2,1,0:T(4,128)S(1)}, u32[]{:S(2)}, u32[]{:S(2)}) collective-permute-start(f32[8,4,640]{2,1,0:T(4,128)S(1)} %get-tuple-element.24), channel_id=1, source_target_pairs={{4,0},{8,4},{12,8},{5,1},{9,5},{13,9},{6,2},{10,6},{14,10},{7,3},{... | collective-permute-start | bytes 245768 | tf_op jit(solution)/shard_map/ppermute | solution.py:187
  96.3 4.6 %collective-permute-start.11 = (f32[8,4,640]{2,1,0:T(4,128)S(1)}, f32[8,4,640]{2,1,0:T(4,128)S(1)}, u32[]{:S(2)}, u32[]{:S(2)}) collective-permute-start(f32[8,4,640]{2,1,0:T(4,128)S(1)} %get-tuple-element.25), channel_id=1, source_target_pairs={{0,4},{4,8},{8,12},{1,5},{5,9},{9,13},{2,6},{6,10},{10,14},{3,7},{... | collective-permute-start | bytes 245768 | tf_op jit(solution)/shard_map/ppermute | solution.py:187
  100.8 0.0 collective-permute-done.9
  100.9 0.5 slice.134
  101.4 0.1 slice.136
  101.5 0.0 collective-permute-done.10
  101.6 1.3 %collective-permute-done.11 = f32[8,4,640]{2,1,0:T(4,128)S(1)} collective-permute-done((f32[8,4,640]{2,1,0:T(4,128)S(1)}, f32[8,4,640]{2,1,0:T(4,128)S(1)}, u32[]{:S(2)}, u32[]{:S(2)}) %collective-permute-start.11) | collective-permute-done | bytes 81952 | tf_op jit(solution)/shard_map/ppermute | solution.py:187
  102.9 0.1 pad_maximum_fusion.1.field_ref
  103.0 4.3 %shard_map.97 = f32[8,16,512]{2,1,0:T(8,128)} custom-call(f32[8,24,640]{2,1,0:T(8,128)S(1)} %pad_maximum_fusion.1.field_ref, f32[9,24,640]{2,1,0:T(8,128)S(1)} %slice.141.extended_ref, f32[8,16,512]{2,1,0:T(8,128)S(1)} %bitcast.36), custom_call_target="tpu_custom_call" | custom-call | tf_op jit(solution)/shard_map/pallas_call | solution.py:260
  (17 shorter events, 0.2 us)
Async XLA Ops:
  7.2 78.0 %reduce-scatter.2.cloned.1.call-start = ((), (), s32[]{:S(2)}) async-start(), calls=%async_computation.1 | async-start | bytes 163840 | tf_op jit(solution)/shard_map/reduce_scatter | solution.py:257
  8.0 12.0 %copy-start = (f32[1,8,16,512]{3,2,1,0:T(8,128)S(1)}, f32[1,8,16,512]{3,2,1,0:T(8,128)}, u32[]{:S(2)}) copy-start(f32[1,8,16,512]{3,2,1,0:T(8,128)} %param.10) | copy-start | bytes 786436
  8.0 12.0 %copy-start.3 = (f32[1,8,16,512]{3,2,1,0:T(8,128)S(1)}, f32[1,8,16,512]{3,2,1,0:T(8,128)}, u32[]{:S(2)}) copy-start(f32[1,8,16,512]{3,2,1,0:T(8,128)} %param.11) | copy-start | bytes 786436
  9.1 8.0 %collective-permute-start = (f32[17,16,4]{2,1,0:T(8,128)S(1)}, f32[17,16,4]{2,1,0:T(8,128)S(1)}, u32[]{:S(2)}, u32[]{:S(2)}) collective-permute-start(f32[17,16,4]{2,1,0:T(8,128)S(1)} %get-tuple-element.22), channel_id=1, source_target_pairs={{1,0},{2,1},{3,2},{0,3},{5,4},{6,5},{7,6},{4,7},{9,8},{10,9},{11,1... | collective-permute-start | bytes 13064 | tf_op jit(solution)/shard_map/ppermute | solution.py:187
  13.0 6.9 %collective-permute-start.1 = (f32[17,16,4]{2,1,0:T(8,128)S(1)}, f32[17,16,4]{2,1,0:T(8,128)S(1)}, u32[]{:S(2)}, u32[]{:S(2)}) collective-permute-start(f32[17,16,4]{2,1,0:T(8,128)S(1)} %get-tuple-element.23), channel_id=1, source_target_pairs={{0,1},{1,2},{2,3},{3,0},{4,5},{5,6},{6,7},{7,4},{8,9},{9,10},{10,1... | collective-permute-start | bytes 13064 | tf_op jit(solution)/shard_map/ppermute | solution.py:187
  20.0 3.0 %copy-start.6 = (s32[1,1,1,4,8192]{4,3,2,1,0:T(4,128)S(1)}, s32[1,1,1,4,8192]{4,3,2,1,0:T(4,128)}, u32[]{:S(2)}) copy-start(s32[1,1,1,4,8192]{4,3,2,1,0:T(4,128)} %param.15) | copy-start | bytes 393220
  20.0 3.0 %copy-start.7 = (s32[1,1,1,4,8192]{4,3,2,1,0:T(4,128)S(1)}, s32[1,1,1,4,8192]{4,3,2,1,0:T(4,128)}, u32[]{:S(2)}) copy-start(s32[1,1,1,4,8192]{4,3,2,1,0:T(4,128)} %param.14) | copy-start | bytes 393220
  20.2 7.4 %collective-permute-start.2 = (f32[17,4,640]{2,1,0:T(4,128)S(1)}, f32[17,4,640]{2,1,0:T(4,128)S(1)}, u32[]{:S(2)}, u32[]{:S(2)}) collective-permute-start(f32[17,4,640]{2,1,0:T(4,128)S(1)} %get-tuple-element.21), channel_id=1, source_target_pairs={{0,3},{1,2},{2,1},{3,0},{4,7},{5,6},{6,5},{7,4},{8,11},{9,10},{10,... | collective-permute-start | bytes 522248 | tf_op jit(solution)/shard_map/ppermute | solution.py:187
  21.7 7.3 %collective-permute-start.3 = (f32[17,4,640]{2,1,0:T(4,128)S(1)}, f32[17,4,640]{2,1,0:T(4,128)S(1)}, u32[]{:S(2)}, u32[]{:S(2)}) collective-permute-start(f32[17,4,640]{2,1,0:T(4,128)S(1)} %get-tuple-element.20), channel_id=1, source_target_pairs={{4,0},{8,4},{12,8},{5,1},{9,5},{13,9},{6,2},{10,6},{14,10},{7,3},{... | collective-permute-start | bytes 522248 | tf_op jit(solution)/shard_map/ppermute | solution.py:187
  23.0 7.5 %collective-permute-start.4 = (f32[17,4,640]{2,1,0:T(4,128)S(1)}, f32[17,4,640]{2,1,0:T(4,128)S(1)}, u32[]{:S(2)}, u32[]{:S(2)}) collective-permute-start(f32[17,4,640]{2,1,0:T(4,128)S(1)} %get-tuple-element.21), channel_id=1, source_target_pairs={{0,4},{4,8},{8,12},{1,5},{5,9},{9,13},{2,6},{6,10},{10,14},{3,7},{... | collective-permute-start | bytes 522248 | tf_op jit(solution)/shard_map/ppermute | solution.py:187
  30.8 3.6 %copy-start.4 = (s32[16,512]{1,0:T(8,128)S(1)}, s32[16,512]{1,0:T(8,128)}, u32[]{:S(2)}) copy-start(s32[16,512]{1,0:T(8,128)} %param.13) | copy-start | bytes 98308
  34.4 0.9 copy-start.5
  34.4 15.8 %copy-start.1 = (f32[1,8,16,512]{3,2,1,0:T(8,128)S(1)}, f32[1,8,16,512]{3,2,1,0:T(8,128)}, u32[]{:S(2)}) copy-start(f32[1,8,16,512]{3,2,1,0:T(8,128)} %param.12) | copy-start | bytes 786436
  34.4 1.3 %collective-permute-start.5 = (f32[64,128]{1,0:T(8,128)S(1)}, f32[64,128]{1,0:T(8,128)S(1)}, u32[]{:S(2)}, u32[]{:S(2)}) collective-permute-start(f32[64,128]{1,0:T(8,128)S(1)} %pad_maximum_fusion.15), channel_id=1, source_target_pairs={{0,16},{16,0},{1,17},{17,1},{2,18},{18,2},{3,19},{19,3},{4,20},{20... | collective-permute-start | bytes 98312 | tf_op jit(solution)/shard_map/ppermute | solution.py:187
  50.2 0.7 copy-start.2
  85.2 1.4 %collective-permute-start.6 = (f32[64,128]{1,0:T(8,128)}, f32[64,128]{1,0:T(8,128)S(1)}, u32[]{:S(2)}, u32[]{:S(2)}) collective-permute-start(f32[64,128]{1,0:T(8,128)} %bitcast.49), channel_id=1, source_target_pairs={{0,16},{16,0},{1,17},{17,1},{2,18},{18,2},{3,19},{19,3},{4,20},{20... | collective-permute-start | bytes 98312 | tf_op jit(solution)/shard_map/ppermute | solution.py:187
  86.7 4.7 %collective-permute-start.7 = (f32[8,16,4]{2,1,0:T(8,128)S(1)}, f32[8,16,4]{2,1,0:T(8,128)S(1)}, u32[]{:S(2)}, u32[]{:S(2)}) collective-permute-start(f32[8,16,4]{2,1,0:T(8,128)S(1)} %get-tuple-element.26), channel_id=1, source_target_pairs={{1,0},{2,1},{3,2},{0,3},{5,4},{6,5},{7,6},{4,7},{9,8},{10,9},{11,1... | collective-permute-start | bytes 6152 | tf_op jit(solution)/shard_map/ppermute | solution.py:187
  89.0 5.2 %collective-permute-start.8 = (f32[8,16,4]{2,1,0:T(8,128)S(1)}, f32[8,16,4]{2,1,0:T(8,128)S(1)}, u32[]{:S(2)}, u32[]{:S(2)}) collective-permute-start(f32[8,16,4]{2,1,0:T(8,128)S(1)} %get-tuple-element.27), channel_id=1, source_target_pairs={{0,1},{1,2},{2,3},{3,0},{4,5},{5,6},{6,7},{7,4},{8,9},{9,10},{10,1... | collective-permute-start | bytes 6152 | tf_op jit(solution)/shard_map/ppermute | solution.py:187
  94.3 6.5 %collective-permute-start.9 = (f32[8,4,640]{2,1,0:T(4,128)S(1)}, f32[8,4,640]{2,1,0:T(4,128)S(1)}, u32[]{:S(2)}, u32[]{:S(2)}) collective-permute-start(f32[8,4,640]{2,1,0:T(4,128)S(1)} %get-tuple-element.25), channel_id=1, source_target_pairs={{0,3},{1,2},{2,1},{3,0},{4,7},{5,6},{6,5},{7,4},{8,11},{9,10},{10,... | collective-permute-start | bytes 245768 | tf_op jit(solution)/shard_map/ppermute | solution.py:187
  95.0 6.5 %collective-permute-start.10 = (f32[8,4,640]{2,1,0:T(4,128)S(1)}, f32[8,4,640]{2,1,0:T(4,128)S(1)}, u32[]{:S(2)}, u32[]{:S(2)}) collective-permute-start(f32[8,4,640]{2,1,0:T(4,128)S(1)} %get-tuple-element.24), channel_id=1, source_target_pairs={{4,0},{8,4},{12,8},{5,1},{9,5},{13,9},{6,2},{10,6},{14,10},{7,3},{... | collective-permute-start | bytes 245768 | tf_op jit(solution)/shard_map/ppermute | solution.py:187
  96.3 6.6 %collective-permute-start.11 = (f32[8,4,640]{2,1,0:T(4,128)S(1)}, f32[8,4,640]{2,1,0:T(4,128)S(1)}, u32[]{:S(2)}, u32[]{:S(2)}) collective-permute-start(f32[8,4,640]{2,1,0:T(4,128)S(1)} %get-tuple-element.25), channel_id=1, source_target_pairs={{0,4},{4,8},{8,12},{1,5},{5,9},{9,13},{2,6},{6,10},{10,14},{3,7},{... | collective-permute-start | bytes 245768 | tf_op jit(solution)/shard_map/ppermute | solution.py:187
Sparse Core Ops, SparseCore 0:
  65.1 20.0 reduce-scatter.1

commit v2 on v1

--- a/solution.py
+++ b/solution.py
@@ -10,6 +10,7 @@
 NSTEP = 4
 LANES = 128
 HALO = 4
+MESH = pl.DeviceIdType.MESH
 
 
 def shifted(value, amount, axis):
@@ -31,36 +32,6 @@
     change = change + south * (shifted(field, 1, 0) - field)
     change = change + north * (shifted(field, -1, 0) - field)
     return field + change
-
-
-def forward_kernel(height, width, field_ref, extended_ref, state_ref):
-    levels = field_ref.shape[0]
-    mask = extended_ref[levels]
-
-    def level(at, carry):
-        coefficients = coefficients_of(extended_ref[at], mask)
-        field = field_ref[at]
-        for _ in range(NSTEP):
-            field = stepped(field, coefficients)
-        state_ref[at] = field[:height, :width]
-        return carry
-
-    lax.fori_loop(0, levels, level, 0)
-
-
-def adjoint_kernel(height, width, field_ref, extended_ref, increment_ref, gradient_ref):
-    levels = field_ref.shape[0]
-    mask = extended_ref[levels]
-
-    def level(at, carry):
-        coefficients = coefficients_of(extended_ref[at], mask)
-        field = field_ref[at]
-        for _ in range(NSTEP):
-            field = stepped(field, coefficients)
-        gradient_ref[at] = field[:height, :width] + increment_ref[at]
-        return carry
-
-    lax.fori_loop(0, levels, level, 0)
 
 
 def table_of(plane):
@@ -183,28 +154,378 @@
     lax.fori_loop(0, bands, backward_band, 0)
 
 
-def over(axis, value, pairs):
-    return lax.ppermute(value, axis, pairs)
-
-
-def extended(cells):
-    lons = lax.axis_size("lon")
-    lats = lax.axis_size("lat")
-    height, width = cells.shape[1:]
-    round_up = [(i, (i + 1) % lons) for i in range(lons)]
-    round_down = [((i + 1) % lons, i) for i in range(lons)]
-    west = over("lon", cells[:, :, width - HALO :], round_up)
-    east = over("lon", cells[:, :, :HALO], round_down)
-    gap = jnp.zeros(cells.shape[:2] + (LANES - 2 * HALO,), cells.dtype)
-    wide = jnp.concatenate([cells, east, gap, west], axis=2)
-    up = [(i, i + 1) for i in range(lats - 1)]
-    down = [(i + 1, i) for i in range(lats - 1)]
-    south = over("lat", wide[:, height - HALO :], up)
-    north = over("lat", wide[:, :HALO], down)
-    mirror = over("lon", wide[:, height - HALO :], [(i, lons - 1 - i) for i in range(lons)])
-    mirror = jnp.roll(mirror[:, ::-1, ::-1], -LANES, axis=2)
-    fold = (lax.axis_index("comp") == 1) & (lax.axis_index("lat") == lats - 1)
-    return jnp.concatenate([wide, jnp.where(fold, mirror, north), south], axis=1)
+def place():
+    comp, lat, lon = (lax.axis_index(name) for name in ("comp", "lat", "lon"))
+    lats, lons = lax.axis_size("lat"), lax.axis_size("lon")
+    return comp, lat, lon, lats, lons
+
+
+def greet(has_south, has_north, at_fold):
+    comp, lat, lon, lats, lons = place()
+    barrier = pltpu.get_barrier_semaphore()
+
+    def hail(*where):
+        pl.semaphore_signal(barrier, inc=1, device_id=where, device_id_type=MESH)
+
+    hail(comp, lat, lax.rem(lon + 1, lons))
+    hail(comp, lat, lax.rem(lon + lons - 1, lons))
+    pl.when(has_south)(lambda: hail(comp, lat - 1, lon))
+    pl.when(has_north)(lambda: hail(comp, lat + 1, lon))
+    pl.when(at_fold)(lambda: hail(comp, lat, lons - 1 - lon))
+
+    def across(band, carry):
+        hail(1 - comp, band, lon)
+        return carry
+
+    lax.fori_loop(0, lats, across, 0)
+    rows = has_south.astype(jnp.int32) + has_north.astype(jnp.int32) + at_fold.astype(jnp.int32)
+    pl.semaphore_wait(barrier, 2 + lats + rows)
+
+
+def edges():
+    comp, lat, lon, lats, lons = place()
+    return lat > 0, lat < lats - 1, (comp == 1) & (lat == lats - 1)
+
+
+def remote(source, target, sems, where):
+    return pltpu.make_async_remote_copy(
+        src_ref=source,
+        dst_ref=target,
+        send_sem=sems[0],
+        recv_sem=sems[1],
+        device_id=where,
+        device_id_type=MESH,
+    )
+
+
+def lon_copies(at, buffers):
+    sent, came, sems = buffers
+    comp, lat, lon, lats, lons = place()
+    ends = (lax.rem(lon + 1, lons), lax.rem(lon + lons - 1, lons))
+    return [
+        remote(
+            sent.at[at, way],
+            came.at[at, way],
+            (sems.at[0, at, way], sems.at[1, at, way]),
+            (comp, lat, ends[way]),
+        )
+        for way in range(2)
+    ]
+
+
+def lon_pack(sent, at, planes):
+    lane = lax.broadcasted_iota(jnp.int32, (planes[0].shape[0], LANES), 1)
+    ahead = jnp.zeros(lane.shape, jnp.float32)
+    behind = jnp.zeros(lane.shape, jnp.float32)
+    for k, plane in enumerate(planes):
+        inside = (lane >= HALO * k) & (lane < HALO * (k + 1))
+        tail = shifted(plane[:, plane.shape[1] - LANES :], HALO * k + HALO, 1)
+        head = shifted(plane[:, :LANES], HALO * k, 1)
+        ahead = jnp.where(inside, tail, ahead)
+        behind = jnp.where(inside, head, behind)
+    sent[at, 0] = ahead
+    sent[at, 1] = behind
+
+
+def lon_unpack(came, at, k):
+    west, east = came[at, 0], came[at, 1]
+    lane = lax.broadcasted_iota(jnp.int32, west.shape, 1)
+    ends = jnp.where(lane >= LANES - HALO, shifted(west, -HALO * (k + 1), 1), 0.0)
+    return jnp.where(lane < HALO, shifted(east, -HALO * k, 1), ends)
+
+
+def mirrored(rows):
+    tiles = []
+    for at in range(0, rows.shape[1], LANES):
+        tile = rows[:, at : at + LANES]
+        for axis, bits in ((1, (1, 2, 4, 8, 16, 32, 64)), (0, (1, 2))):
+            index = lax.broadcasted_iota(jnp.int32, tile.shape, axis)
+            for bit in bits:
+                odd = lax.rem(index // bit, 2) == 1
+                tile = jnp.where(odd, shifted(tile, bit, axis), shifted(tile, -bit, axis))
+        tiles.append(tile)
+    own = tiles[-2::-1]
+    return jnp.concatenate(own + tiles[-1:], axis=1)
+
+
+def lat_copies(at, buffers):
+    sent, came, sems = buffers
+    comp, lat, lon, lats, lons = place()
+    has_south, has_north, at_fold = edges()
+
+    def one(way, slot, where):
+        return remote(
+            sent.at[at, way],
+            came.at[at, slot],
+            (sems.at[0, at, way], sems.at[1, at, slot]),
+            where,
+        )
+
+    return (
+        (has_north, one(0, 0, (comp, lat + 1, lon))),
+        (has_south, one(1, 1, (comp, lat - 1, lon))),
+        (at_fold, one(0, 1, (comp, lat, lons - 1 - lon))),
+    )
+
+
+def lat_start(at, buffers):
+    for there, copy in lat_copies(at, buffers):
+        pl.when(there)(copy.start)
+
+
+def lat_sent(at, buffers):
+    for there, copy in lat_copies(at, buffers):
+        pl.when(there)(copy.wait_send)
+
+
+def lat_came(at, buffers):
+    came = buffers[1]
+    has_south, has_north, at_fold = edges()
+    up, down, fold = (copy for there, copy in lat_copies(at, buffers))
+    pl.when(has_south)(up.wait_recv)
+    pl.when(has_north)(down.wait_recv)
+    pl.when(at_fold)(fold.wait_recv)
+
+    @pl.when(at_fold)
+    def _():
+        came[at, 1] = mirrored(came[at, 1])
+
+    @pl.when(jnp.logical_not(has_south))
+    def _():
+        came[at, 0] = jnp.zeros(came.shape[2:], jnp.float32)
+
+    @pl.when(jnp.logical_not(has_north | at_fold))
+    def _():
+        came[at, 1] = jnp.zeros(came.shape[2:], jnp.float32)
+
+    south, north = came[at, 0], came[at, 1]
+    upper = jnp.concatenate([north[:HALO], south[:HALO]], axis=0)
+    lower = jnp.concatenate([north[HALO:], south[HALO:]], axis=0)
+    return upper, lower
+
+
+def lat_pack(sent, at, first, second):
+    top = first.shape[0] - HALO
+    sent[at, 0] = jnp.concatenate([first[top:], second[top:]], axis=0)
+    sent[at, 1] = jnp.concatenate([first[:HALO], second[:HALO]], axis=0)
+
+
+def band_copies(source, came, sems):
+    comp, lat, lon, lats, lons = place()
+
+    def one(band):
+        return remote(
+            source(band), came.at[lat], (sems.at[0, band], sems.at[1, lat]), (1 - comp, band, lon)
+        )
+
+    def arrival(band):
+        return remote(
+            source(band), came.at[band], (sems.at[0, band], sems.at[1, band]), (1 - comp, band, lon)
+        )
+
+    def each(act):
+        def body(band, carry):
+            act(band)
+            return carry
+
+        lax.fori_loop(0, lats, body, 0)
+
+    return (
+        lambda: each(lambda band: one(band).start()),
+        lambda: each(lambda band: arrival(band).wait_recv()),
+        lambda: each(lambda band: one(band).wait_send()),
+    )
+
+
+def forward_kernel(
+    increment_ref,
+    diffusivity_ref,
+    land_ref,
+    state_ref,
+    fixed_ref,
+    source_ref,
+    field,
+    surface,
+    surfaces,
+    lon_sent,
+    lon_came,
+    lat_sent_ref,
+    lat_came_ref,
+    lon_sems,
+    lat_sems,
+    band_sems,
+):
+    levels, height, width = increment_ref.shape
+    greet(*edges())
+    ocean = lax.axis_index("comp") == 1
+    mask = jnp.where(ocean, land_ref[...].astype(jnp.float32), 1.0)
+    lons = (lon_sent, lon_came, lon_sems)
+    lats = (lat_sent_ref, lat_came_ref, lat_sems)
+    planes = [increment_ref[k] for k in range(levels)]
+    planes = planes + [diffusivity_ref[k] for k in range(levels)] + [mask]
+    lon_pack(lon_sent, 0, planes)
+    for copy in lon_copies(0, lons):
+        copy.start()
+    own = pl.ds(0, height), pl.ds(0, width)
+    side = pl.ds(0, height), pl.ds(width, LANES)
+    fixed_ref[(levels,) + own] = mask
+
+    def fill(k, carry):
+        field[(k,) + own] = increment_ref[k]
+        fixed_ref[(k,) + own] = diffusivity_ref[k]
+        return carry
+
+    lax.fori_loop(0, levels, fill, 0)
+    for copy in lon_copies(0, lons):
+        copy.wait_recv()
+    for k in range(levels):
+        field[(k,) + side] = lon_unpack(lon_came, 0, k)
+        fixed_ref[(k,) + side] = lon_unpack(lon_came, 0, levels + k)
+    fixed_ref[(levels,) + side] = lon_unpack(lon_came, 0, 2 * levels)
+
+    wide_mask = fixed_ref[levels, pl.ds(0, height), :]
+    lat_pack(lat_sent_ref, levels, wide_mask, wide_mask)
+    lat_start(levels, lats)
+
+    def send(k, carry):
+        rows = pl.ds(0, height)
+        lat_pack(lat_sent_ref, k, field[k, rows, :], fixed_ref[k, rows, :])
+        lat_start(k, lats)
+        return carry
+
+    lax.fori_loop(0, levels, send, 0)
+    ends = pl.ds(height, 2 * HALO)
+    fixed_ref[levels, ends, :] = lat_came(levels, lats)[0]
+
+    def level(k):
+        field[k, ends, :], fixed_ref[k, ends, :] = lat_came(k, lats)
+        coefficients = coefficients_of(fixed_ref[k], fixed_ref[levels])
+        value = field[k]
+        for _ in range(NSTEP):
+            value = stepped(value, coefficients)
+        state_ref[k] = value[:height, :width]
+
+    level(0)
+    surface[...] = table_of(mask * state_ref[0])
+    start, arrive, finish = band_copies(lambda band: surface, surfaces, band_sems)
+    start()
+
+    def rest(k, carry):
+        level(k)
+        return carry
+
+    lax.fori_loop(1, levels, rest, 0)
+    for copy in lon_copies(0, lons):
+        copy.wait_send()
+
+    def drain(k, carry):
+        lat_sent(k, lats)
+        return carry
+
+    lax.fori_loop(0, levels + 1, drain, 0)
+    arrive()
+    source_ref[...] = surfaces[...]
+    finish()
+
+
+def adjoint_kernel(
+    adjoint_ref,
+    sums_ref,
+    fixed_ref,
+    increment_ref,
+    gradient_ref,
+    field,
+    returns,
+    lon_sent,
+    lon_came,
+    lat_sent_ref,
+    lat_came_ref,
+    lon_sems,
+    lat_sems,
+    band_sems,
+):
+    levels, height, width = increment_ref.shape
+    pairs = levels // 2
+    greet(*edges())
+    start, arrive, finish = band_copies(lambda band: sums_ref.at[band], returns, band_sems)
+    start()
+    lons = (lon_sent, lon_came, lon_sems)
+    lats = (lat_sent_ref, lat_came_ref, lat_sems)
+    rows = pl.ds(0, height)
+    own = rows, pl.ds(0, width)
+    side = rows, pl.ds(width, LANES)
+    ends = pl.ds(height, 2 * HALO)
+    lon_pack(lon_sent, 0, [adjoint_ref[k] for k in range(1, levels)])
+    for copy in lon_copies(0, lons):
+        copy.start()
+
+    def fill(k, carry):
+        field[(k,) + own] = adjoint_ref[k]
+        return carry
+
+    lax.fori_loop(1, levels, fill, 0)
+    for copy in lon_copies(0, lons):
+        copy.wait_recv()
+    for k in range(1, levels):
+        field[(k,) + side] = lon_unpack(lon_came, 0, k - 1)
+
+    def send(pair, carry):
+        first = field[2 * pair - 1, rows, :]
+        second = field[jnp.minimum(2 * pair, levels - 1), rows, :]
+        lat_pack(lat_sent_ref, pair, first, second)
+        lat_start(pair, lats)
+        return carry
+
+    lax.fori_loop(1, pairs + 1, send, 0)
+    arrive()
+
+    def add(band, total):
+        return total + returns[band]
+
+    total = lax.fori_loop(1, returns.shape[0], add, returns[0])
+    mask = fixed_ref[(levels,) + own]
+    first = adjoint_ref[0] + mask * plane_of(total, height)
+    lon_pack(lon_sent, 1, [first])
+    for copy in lon_copies(1, lons):
+        copy.start()
+    field[(0,) + own] = first
+
+    def sweep(k):
+        coefficients = coefficients_of(fixed_ref[k], fixed_ref[levels])
+        value = field[k]
+        for _ in range(NSTEP):
+            value = stepped(value, coefficients)
+        gradient_ref[k] = value[:height, :width] + increment_ref[k]
+
+    for copy in lon_copies(1, lons):
+        copy.wait_recv()
+    field[(0,) + side] = lon_unpack(lon_came, 1, 0)
+    wide = field[0, rows, :]
+    lat_pack(lat_sent_ref, 0, wide, wide)
+    lat_start(0, lats)
+
+    def couple_of(pair, carry):
+        later = jnp.minimum(2 * pair, levels - 1)
+        upper, lower = lat_came(pair, lats)
+        field[later, ends, :] = lower
+        field[2 * pair - 1, ends, :] = upper
+        sweep(2 * pair - 1)
+        pl.when(2 * pair < levels)(lambda: sweep(later))
+        return carry
+
+    lax.fori_loop(1, pairs + 1, couple_of, 0)
+    field[0, ends, :] = lat_came(0, lats)[0]
+    sweep(0)
+    for at in range(2):
+        for copy in lon_copies(at, lons):
+            copy.wait_send()
+
+    def drain(k, carry):
+        lat_sent(k, lats)
+        return carry
+
+    lax.fori_loop(0, pairs + 1, drain, 0)
+    finish()
 
 
 def local(
@@ -213,37 +534,51 @@
     levels, height, width = increment.shape[1:]
     bands = lax.axis_size("lat")
     rows = height * width // LANES
-    capacity = pull_cells.shape[-1]
-    lines = capacity // LANES
+    lines = pull_cells.shape[-1] // LANES
+    tall, wide = height + 2 * HALO, width + LANES
+    pairs = levels // 2
     ocean = lax.axis_index("comp") == 1
     mask = jnp.where(ocean, land_mask.astype(jnp.float32), jnp.ones(land_mask.shape, jnp.float32))
     whole = pl.BlockSpec(memory_space=pltpu.VMEM)
-    params = pltpu.CompilerParams(vmem_limit_bytes=48 * 1024 * 1024)
-    block = jax.ShapeDtypeStruct((levels, height, width), jnp.float32)
-
-    fixed = jnp.concatenate([diffusivity[0], mask[None]], axis=0)
-    both = extended(jnp.concatenate([increment[0], fixed], axis=0))
-    state = pl.pallas_call(
-        functools.partial(forward_kernel, height, width),
-        out_shape=block,
-        in_specs=[whole, whole],
-        out_specs=whole,
-        compiler_params=params,
-    )(both[:levels], both[levels:])
-
-    surface = table_of(mask * state[0])
-    swap = [(0, 1), (1, 0)]
-    source = lax.all_gather(over("comp", surface, swap), "lat", axis=0, tiled=False)
+    space = 48 * 1024 * 1024
+
+    def real(*shape):
+        return jax.ShapeDtypeStruct(shape, jnp.float32)
+
+    def room(*shape):
+        return pltpu.VMEM(shape, jnp.float32)
+
+    def halos(sides, messages):
+        return [
+            room(sides, 2, height, LANES),
+            room(sides, 2, height, LANES),
+            room(messages, 2, 2 * HALO, wide),
+            room(messages, 2, 2 * HALO, wide),
+            pltpu.SemaphoreType.DMA((2, sides, 2)),
+            pltpu.SemaphoreType.DMA((2, messages, 2)),
+            pltpu.SemaphoreType.DMA((2, bands)),
+        ]
+
+    block = real(levels, height, width)
+    state, fixed, source = pl.pallas_call(
+        forward_kernel,
+        out_shape=(block, real(levels + 1, tall, wide), real(bands, rows, LANES)),
+        in_specs=[whole] * 3,
+        out_specs=(whole,) * 3,
+        scratch_shapes=[room(levels, tall, wide), room(rows, LANES), room(bands, rows, LANES)]
+        + halos(1, levels + 1),
+        compiler_params=pltpu.CompilerParams(
+            vmem_limit_bytes=space, collective_id=0, has_side_effects=True
+        ),
+    )(increment[0], diffusivity[0], land_mask)
+
     linear, adjoint, sums = pl.pallas_call(
         functools.partial(couple_kernel, height, width),
-        out_shape=(block, block, jax.ShapeDtypeStruct((bands, rows, LANES), jnp.float32)),
+        out_shape=(block, block, real(bands, rows, LANES)),
         in_specs=[pl.BlockSpec(memory_space=pltpu.SMEM)] + [whole] * 7,
         out_specs=(whole, whole, whole),
-        scratch_shapes=[
-            pltpu.VMEM((2 * rows, LANES), jnp.float32),
-            pltpu.VMEM((rows, LANES), jnp.float32),
-        ],
-        compiler_params=params,
+        scratch_shapes=[room(2 * rows, LANES), room(rows, LANES)],
+        compiler_params=pltpu.CompilerParams(vmem_limit_bytes=space),
     )(
         pull_count.reshape(bands),
         source,
@@ -254,16 +589,18 @@
         state,
         innovation[0],
     )
-    band_sums = lax.psum_scatter(sums, "lat", scatter_dimension=0, tiled=False)
-    returned = plane_of(over("comp", band_sums, swap), height)
-    adjoint = adjoint.at[0].add(mask * returned)
+
     gradient = pl.pallas_call(
-        functools.partial(adjoint_kernel, height, width),
+        adjoint_kernel,
         out_shape=block,
-        in_specs=[whole, whole, whole],
+        in_specs=[whole] * 4,
         out_specs=whole,
-        compiler_params=params,
-    )(extended(adjoint), both[levels:], increment[0])
+        scratch_shapes=[room(levels, tall, wide), room(bands, rows, LANES)]
+        + halos(2, pairs + 1),
+        compiler_params=pltpu.CompilerParams(
+            vmem_limit_bytes=space, collective_id=1, has_side_effects=True
+        ),
+    )(adjoint, sums, fixed, increment[0])
     return (linear[None], gradient[None])
 
 

time: 114 us -> 50.9 us (0.45)
  waiting for transfers between devices: 37.5 us -> 0 us
  Pallas kernels: 22 us -> 45.9 us
  starting transfers between devices: 20.2 us -> 0 us
  blocking collectives: 14.5 us -> 0 us
  between operations: 14.4 us -> 0.72 us
  other arithmetic: 2.54 us -> 0.8 us
    pallas_call x2, Pallas kernels: 7.84 us -> 31.8 us  [the longest x1 16.7 us: local(): pl.pallas_call(forward_kernel, out_shape=(block, real(levels + 1, tall, w...]
    reduce_scatter x1 -> x0, waiting for transfers between devices: 20.2 us -> none  [local(): band_sums = lax.psum_scatter(sums, 'lat', scatter_dimension=0, tiled=False)]
    ppermute x12 -> x0, starting transfers between devices: 20.2 us -> none  [over(): return lax.ppermute(value, axis, pairs)]
    ppermute x12 -> x0, waiting for transfers between devices: 17.3 us -> none  [over(): return lax.ppermute(value, axis, pairs)]
    all_gather x1 -> x0, blocking collectives: 14.5 us -> none  [local(): lax.all_gather(over('comp', surface, swap), 'lat', axis=0, tiled=False)]
    unnamed x17 -> x16, local copies, waits for them, and re-layouts: 1.45 us -> 3.3 us
    slice x13 -> x0, local copies, waits for them, and re-layouts: 1.57 us -> none  [the longest x8 1.4 us: extended(): mirror = jnp.roll(mirror[:, ::-1, ::-1], -LANES, axis=2)]
  transfers between devices with their start and end apart: 13 -> 0, of which waited for: 10 -> 0; matrix products, arithmetic and copies ran while one was open for 1% -> 0% of each run, Pallas kernels for 0% -> 0%
where the time goes in v2:
time: 50.9 us; the launch traced here: 50.7 us
  Pallas kernels  45.9 us (90%)
  local copies, waits for them, and re-layouts  3.32 us (7%)
  other arithmetic  0.8 us (2%)
  between operations  0.72 us (1%)
    pallas_call x1, Pallas kernels, local(): pl.pallas_call(forward_kernel, out_shape=(block, real(levels + 1, tall, w...  16.7 us
    pallas_call x1, Pallas kernels, local(): pl.pallas_call(adjoint_kernel, out_shape=block, in_specs=[whole] * 4, out...  15.2 us
    pallas_call x1, Pallas kernels, local(): pl.pallas_call(functools.partial(couple_kernel, height, width), out_shape...  14.1 us
    unnamed x16, local copies, waits for them, and re-layouts  3.3 us

profile of v2, /device:TPU:0, one launch (start us, length us, event | category | flops | bytes accessed | tf_op | source)
XLA Modules:
  0.0 50.7 jit_solution(10936979077507949243)
XLA Ops:
  0.6 0.0 copy-start.6
  0.6 0.8 %convert_select_fusion.mask_ref = f32[16,512]{1,0:T(8,128)S(1)} fusion(s32[16,512]{1,0:T(8,128)} %land_ref.1, pred[]{:T(512)S(6)} %eq.3), kind=kLoop, calls=%fused_computation.3 | loop fusion | flops 16384 | bytes 65537 | tf_op jit(solution)/shard_map/jit(_where)/select_n | solution.py:541
  1.4 0.0 copy-start.5
  1.4 0.0 copy-start.3
  1.4 0.9 %copy.16 = f32[1,4,64,128]{3,2,1,0:T(8,128)S(1)} copy(f32[1,4,64,128]{3,1,2,0:T(4,128)} %bitcast.26) | data formatting | bytes 262144
  2.4 0.0 copy-done.6
  2.4 0.0 copy-done.5
  2.4 0.0 copy-start
  2.4 0.0 copy-start.1
  2.5 0.0 copy-done.3
  2.5 0.9 %copy-done = f32[1,8,16,512]{3,2,1,0:T(8,128)S(1)} copy-done((f32[1,8,16,512]{3,2,1,0:T(8,128)S(1)}, f32[1,8,16,512]{3,2,1,0:T(8,128)}, u32[]{:S(2)}) %copy-start) | copy-done | bytes 262168
  3.4 0.1 copy-done.1
  3.5 0.0 copy-start.2
  3.5 16.7 %shard_map.95 = (f32[8,16,512]{2,1,0:T(8,128)S(1)}, f32[9,24,640]{2,1,0:T(8,128)S(1)}, f32[4,64,128]{2,1,0:T(8,128)S(1)}) custom-call(f32[8,16,512]{2,1,0:T(8,128)S(1)} %bitcast.19, f32[8,16,512]{2,1,0:T(8,128)S(1)} %bitcast.23, s32[16,512]{1,0:T(8,128)S(1)} %copy-done.3), custom_call_target="tpu_custom_call" | custom-call | tf_op jit(solution)/shard_map/pallas_call | solution.py:563
  20.1 0.0 copy-start.4
  20.1 0.0 copy-done.2
  20.1 0.6 %copy-done.4 = s32[1,1,1,4]{3,2,1,0:T(1,128)S(1)} copy-done((s32[1,1,1,4]{3,2,1,0:T(1,128)S(1)}, s32[1,1,1,4]{3,2,1,0:T(1,128)}, u32[]{:S(2)}) %copy-start.4) | copy-done | bytes 40
  20.8 14.1 %shard_map.96 = (f32[8,16,512]{2,1,0:T(8,128)}, f32[8,16,512]{2,1,0:T(8,128)S(1)}, f32[4,64,128]{2,1,0:T(8,128)S(1)}) custom-call(s32[4]{0:T(128)S(1)} %bitcast.25, f32[4,64,128]{2,1,0:T(8,128)S(1)} %get-tuple-element.8.source_ref, s32[4,64,128]{2,1,0:T(8,128)S(1)} %get-tuple-element.15.pull_ref, s32[4,64,128]{2,1,0:T(8,128)S(1)} %get-tuple-element.14.put_ref, ...), custom_call_target="tpu_custom_call" | custom-call | tf_op jit(solution)/shard_map/pallas_call | solution.py:575
  34.9 15.2 %shard_map.97 = f32[8,16,512]{2,1,0:T(8,128)S(1)} custom-call(f32[8,16,512]{2,1,0:T(8,128)S(1)} %get-tuple-element.11.adjoint_ref, f32[4,64,128]{2,1,0:T(8,128)S(1)} %get-tuple-element.12.sums_ref, f32[9,24,640]{2,1,0:T(8,128)S(1)} %get-tuple-element.13.fixed_ref, f32[8,16,512]{2,1,0:T(8,128)S(1)} %bitcast.20), custom_call_target="tpu_custom_call" | custom-call | tf_op jit(solution)/shard_map/pallas_call | solution.py:593
  50.0 0.7 %copy.18 = f32[1,8,16,512]{3,2,1,0:T(8,128)} copy(f32[1,8,16,512]{3,2,1,0:T(8,128)S(1)} %bitcast.21) | data formatting | bytes 524288
  (1 shorter events, 0.0 us)
Async XLA Ops:
  0.6 1.8 %copy-start.6 = (s32[1,1,1,4,8192]{4,3,2,1,0:T(4,128)S(1)}, s32[1,1,1,4,8192]{4,3,2,1,0:T(4,128)}, u32[]{:S(2)}) copy-start(s32[1,1,1,4,8192]{4,3,2,1,0:T(4,128)} %param.12) | copy-start | bytes 393220
  1.4 1.0 %copy-start.5 = (s32[1,1,1,4,8192]{4,3,2,1,0:T(4,128)S(1)}, s32[1,1,1,4,8192]{4,3,2,1,0:T(4,128)}, u32[]{:S(2)}) copy-start(s32[1,1,1,4,8192]{4,3,2,1,0:T(4,128)} %param.13) | copy-start | bytes 393220
  1.4 1.0 %copy-start.3 = (s32[16,512]{1,0:T(8,128)S(1)}, s32[16,512]{1,0:T(8,128)}, u32[]{:S(2)}) copy-start(s32[16,512]{1,0:T(8,128)} %land_ref.1) | copy-start | bytes 98308
  2.4 0.9 %copy-start = (f32[1,8,16,512]{3,2,1,0:T(8,128)S(1)}, f32[1,8,16,512]{3,2,1,0:T(8,128)}, u32[]{:S(2)}) copy-start(f32[1,8,16,512]{3,2,1,0:T(8,128)} %param.8) | copy-start | bytes 786436
  2.4 1.0 %copy-start.1 = (f32[1,8,16,512]{3,2,1,0:T(8,128)S(1)}, f32[1,8,16,512]{3,2,1,0:T(8,128)}, u32[]{:S(2)}) copy-start(f32[1,8,16,512]{3,2,1,0:T(8,128)} %param.9) | copy-start | bytes 786436
  3.5 16.7 %copy-start.2 = (f32[1,8,16,512]{3,2,1,0:T(8,128)S(1)}, f32[1,8,16,512]{3,2,1,0:T(8,128)}, u32[]{:S(2)}) copy-start(f32[1,8,16,512]{3,2,1,0:T(8,128)} %param.10) | copy-start | bytes 786436
  20.1 0.7 %copy-start.4 = (s32[1,1,1,4]{3,2,1,0:T(1,128)S(1)}, s32[1,1,1,4]{3,2,1,0:T(1,128)}, u32[]{:S(2)}) copy-start(s32[1,1,1,4]{3,2,1,0:T(1,128)} %param.15) | copy-start | bytes 52

commit v3 on v2

--- a/solution.py
+++ b/solution.py
@@ -56,7 +56,7 @@
 
     def one(row, found):
         line = jnp.broadcast_to(table_ref[index + (pl.ds(row, 1), slice(None))], low.shape)
-        return jnp.where(high == row, jnp.take_along_axis(line, low, axis=1), found)
+        return jnp.where(high == row, jnp.take_along_axis(line, low, axis=1, mode="promise_in_bounds"), found)
 
     found = jnp.zeros(low.shape, jnp.float32)
     for row in range(rows):
@@ -65,17 +65,25 @@
 
 
 def spread(values, high, low, rows):
-    first = values.astype(jnp.bfloat16).astype(jnp.float32)
+    narrow = jnp.bfloat16
+    pack = 16
+
+    def lined(row, count):
+        tile = jnp.broadcast_to(row.astype(jnp.float32), (pack, LANES)).astype(narrow)
+        return jnp.concatenate([tile] * (count // pack), axis=0)
+
+    first = values.astype(narrow).astype(jnp.float32)
     second = values - first
-    row_at = lax.broadcasted_iota(jnp.int32, (rows, LANES), 0)
-    lane_at = lax.broadcasted_iota(jnp.int32, (LANES, LANES), 0)
+    row_at = lax.broadcasted_iota(jnp.int32, (rows, LANES), 0).astype(jnp.float32).astype(narrow)
+    lane_at = lax.broadcasted_iota(jnp.int32, (LANES, LANES), 0).astype(jnp.float32).astype(narrow)
+    one, zero = jnp.ones((), narrow), jnp.zeros((), narrow)
     left, right = [], []
     for r in range(values.shape[0]):
-        hit = high[r : r + 1] == row_at
-        top = jnp.where(hit, first[r : r + 1], 0.0).astype(jnp.bfloat16)
-        bottom = jnp.where(hit, second[r : r + 1], 0.0).astype(jnp.bfloat16)
+        hit = lined(high[r : r + 1], rows) == row_at
+        top = jnp.where(hit, lined(first[r : r + 1], rows), zero)
+        bottom = jnp.where(hit, lined(second[r : r + 1], rows), zero)
         left.append(jnp.concatenate([top, bottom], axis=0))
-        right.append(jnp.where(low[r : r + 1] == lane_at, 1.0, 0.0).astype(jnp.bfloat16))
+        right.append(jnp.where(lined(low[r : r + 1], LANES) == lane_at, one, zero))
     return lax.dot_general(
         jnp.concatenate(left, axis=1),
         jnp.concatenate(right, axis=1),
@@ -92,7 +100,7 @@
     pull_ref,
     put_ref,
     weight_ref,
-    mask_ref,
+    land_ref,
     state_ref,
     innovation_ref,
     linear_ref,
@@ -104,7 +112,7 @@
     bands = source_ref.shape[0]
     lines = pull_ref.shape[1]
     rows = height * width // LANES
-    deep = min(8, lines)
+    deep = min(16, lines)
     block = deep * LANES
     slot = lax.broadcasted_iota(jnp.int32, (deep, LANES), 0) * LANES
     slot = slot + lax.broadcasted_iota(jnp.int32, (deep, LANES), 1)
@@ -131,7 +139,8 @@
         return lax.fori_loop(0, blocks(band), body, carry)
 
     lax.fori_loop(0, bands, forward_band, 0)
-    mask = mask_ref[...]
+    ocean = lax.axis_index("comp") == 1
+    mask = jnp.where(ocean, land_ref[...].astype(jnp.float32), 1.0)
     income = plane_of(total_ref[:rows] + total_ref[rows:], height)
     linear_ref[...] = state_ref[...]
     linear_ref[0] = state_ref[0] + mask * income
@@ -537,8 +546,6 @@
     lines = pull_cells.shape[-1] // LANES
     tall, wide = height + 2 * HALO, width + LANES
     pairs = levels // 2
-    ocean = lax.axis_index("comp") == 1
-    mask = jnp.where(ocean, land_mask.astype(jnp.float32), jnp.ones(land_mask.shape, jnp.float32))
     whole = pl.BlockSpec(memory_space=pltpu.VMEM)
     space = 48 * 1024 * 1024
 
@@ -585,7 +592,7 @@
         pull_cells.reshape(bands, lines, LANES),
         put_cells.reshape(bands, lines, LANES),
         pull_weight.reshape(bands, lines, LANES),
-        mask,
+        land_mask,
         state,
         innovation[0],
     )

time: 50.9 us -> 46.3 us (0.910)
  Pallas kernels: 45.9 us -> 41.9 us
  other arithmetic: 0.8 us -> 0 us
    pallas_call x1, Pallas kernels: 14.1 us -> 10.8 us  [local(): pl.pallas_call(functools.partial(couple_kernel, height, width), out_shape...]
    reshape x1, local copies, waits for them, and re-layouts: 0.02 us -> 0.98 us  [local(): put_cells.reshape(bands, lines, LANES)]
    unnamed x16 -> x14, local copies, waits for them, and re-layouts: 3.3 us -> 2.39 us
    pallas_call x1, Pallas kernels: 15.2 us -> 14.4 us  [local(): pl.pallas_call(adjoint_kernel, out_shape=block, in_specs=[whole] * 4, out...]
    select_n x1 -> x0, other arithmetic: 0.8 us -> none  [local(): jnp.where(ocean, land_mask.astype(jnp.float32), jnp.ones(land_mask.shape,...]
where the time goes in v3:
time: 46.3 us; the launch traced here: 46 us
  Pallas kernels  41.9 us (90%)
  local copies, waits for them, and re-layouts  3.37 us (7%)
  between operations  0.73 us (2%)
    pallas_call x1, Pallas kernels, local(): pl.pallas_call(forward_kernel, out_shape=(block, real(levels + 1, tall, w...  16.7 us
    pallas_call x1, Pallas kernels, local(): pl.pallas_call(adjoint_kernel, out_shape=block, in_specs=[whole] * 4, out...  14.4 us
    pallas_call x1, Pallas kernels, local(): pl.pallas_call(functools.partial(couple_kernel, height, width), out_shape...  10.8 us
    unnamed x14, local copies, waits for them, and re-layouts  2.39 us
    reshape x1, local copies, waits for them, and re-layouts, local(): put_cells.reshape(bands, lines, LANES)  0.98 us

profile of v3, /device:TPU:0, one launch (start us, length us, event | category | flops | bytes accessed | tf_op | source)
XLA Modules:
  0.0 46.0 jit_solution(11442859395129206438)
XLA Ops:
  0.6 0.0 copy-start.5
  0.6 0.0 copy-start.3
  0.7 0.9 %copy.16 = f32[1,4,64,128]{3,2,1,0:T(8,128)S(1)} copy(f32[1,4,64,128]{3,1,2,0:T(4,128)} %bitcast.26) | data formatting | bytes 262144
  1.6 0.0 copy-done.5
  1.6 0.0 copy-start
  1.6 0.0 copy-start.1
  1.6 1.0 %copy_bitcast_fusion.1 = (s32[4,64,128]{2,1,0:T(8,128)S(1)}, s32[4,64,128]{2,1,0:T(8,128)S(1)}) fusion(s32[1,4,64,128]{3,1,2,0:T(4,128)S(1)} %bitcast.27, s32[1,4,64,128]{3,1,2,0:T(4,128)} %bitcast.28), kind=kLoop, calls=%fused_computation.1 | loop fusion | bytes 524288 | tf_op jit(solution)/shard_map/reshape | solution.py:593
  2.6 0.0 copy-done.3
  2.6 0.0 copy-done
  2.6 0.1 copy-done.1
  2.7 0.0 copy-start.2
  2.7 16.7 %shard_map.95 = (f32[8,16,512]{2,1,0:T(8,128)S(1)}, f32[9,24,640]{2,1,0:T(8,128)S(1)}, f32[4,64,128]{2,1,0:T(8,128)S(1)}) custom-call(f32[8,16,512]{2,1,0:T(8,128)S(1)} %bitcast.19, f32[8,16,512]{2,1,0:T(8,128)S(1)} %bitcast.23, s32[16,512]{1,0:T(8,128)S(1)} %copy-done.3), custom_call_target="tpu_custom_call" | custom-call | tf_op jit(solution)/shard_map/pallas_call | solution.py:570
  19.4 0.0 copy-start.4
  19.4 0.0 copy-done.2
  19.4 0.6 %copy-done.4 = s32[1,1,1,4]{3,2,1,0:T(1,128)S(1)} copy-done((s32[1,1,1,4]{3,2,1,0:T(1,128)S(1)}, s32[1,1,1,4]{3,2,1,0:T(1,128)}, u32[]{:S(2)}) %copy-start.4) | copy-done | bytes 40
  20.1 10.8 %shard_map.96 = (f32[8,16,512]{2,1,0:T(8,128)}, f32[8,16,512]{2,1,0:T(8,128)S(1)}, f32[4,64,128]{2,1,0:T(8,128)S(1)}) custom-call(s32[4]{0:T(128)S(1)} %bitcast.25, f32[4,64,128]{2,1,0:T(8,128)S(1)} %get-tuple-element.8.source_ref, s32[4,64,128]{2,1,0:T(8,128)S(1)} %get-tuple-element.15.pull_ref, s32[4,64,128]{2,1,0:T(8,128)S(1)} %get-tuple-element.14.put_ref, ...), custom_call_target="tpu_custom_call" | custom-call | tf_op jit(solution)/shard_map/pallas_call | solution.py:582
  30.9 14.4 %shard_map.97 = f32[8,16,512]{2,1,0:T(8,128)S(1)} custom-call(f32[8,16,512]{2,1,0:T(8,128)S(1)} %get-tuple-element.11.adjoint_ref, f32[4,64,128]{2,1,0:T(8,128)S(1)} %get-tuple-element.12.sums_ref, f32[9,24,640]{2,1,0:T(8,128)S(1)} %get-tuple-element.13.fixed_ref, f32[8,16,512]{2,1,0:T(8,128)S(1)} %bitcast.20), custom_call_target="tpu_custom_call" | custom-call | tf_op jit(solution)/shard_map/pallas_call | solution.py:600
  45.3 0.7 %copy.18 = f32[1,8,16,512]{3,2,1,0:T(8,128)} copy(f32[1,8,16,512]{3,2,1,0:T(8,128)S(1)} %bitcast.21) | data formatting | bytes 524288
Async XLA Ops:
  0.6 1.0 %copy-start.5 = (s32[1,1,1,4,8192]{4,3,2,1,0:T(4,128)S(1)}, s32[1,1,1,4,8192]{4,3,2,1,0:T(4,128)}, u32[]{:S(2)}) copy-start(s32[1,1,1,4,8192]{4,3,2,1,0:T(4,128)} %param.13) | copy-start | bytes 393220
  0.6 2.0 %copy-start.3 = (s32[16,512]{1,0:T(8,128)S(1)}, s32[16,512]{1,0:T(8,128)}, u32[]{:S(2)}) copy-start(s32[16,512]{1,0:T(8,128)} %land_ref.3) | copy-start | bytes 98308
  1.6 1.0 %copy-start = (f32[1,8,16,512]{3,2,1,0:T(8,128)S(1)}, f32[1,8,16,512]{3,2,1,0:T(8,128)}, u32[]{:S(2)}) copy-start(f32[1,8,16,512]{3,2,1,0:T(8,128)} %param.8) | copy-start | bytes 786436
  1.6 1.1 %copy-start.1 = (f32[1,8,16,512]{3,2,1,0:T(8,128)S(1)}, f32[1,8,16,512]{3,2,1,0:T(8,128)}, u32[]{:S(2)}) copy-start(f32[1,8,16,512]{3,2,1,0:T(8,128)} %param.9) | copy-start | bytes 786436
  2.7 16.7 %copy-start.2 = (f32[1,8,16,512]{3,2,1,0:T(8,128)S(1)}, f32[1,8,16,512]{3,2,1,0:T(8,128)}, u32[]{:S(2)}) copy-start(f32[1,8,16,512]{3,2,1,0:T(8,128)} %param.10) | copy-start | bytes 786436
  19.4 0.7 %copy-start.4 = (s32[1,1,1,4]{3,2,1,0:T(1,128)S(1)}, s32[1,1,1,4]{3,2,1,0:T(1,128)}, u32[]{:S(2)}) copy-start(s32[1,1,1,4]{3,2,1,0:T(1,128)} %param.15) | copy-start | bytes 52

commit v4 on v3

--- a/solution.py
+++ b/solution.py
@@ -121,11 +121,11 @@
         where = pl.ds(pl.multiple_of(at * deep, deep), deep)
         pull = split_cell(pull_ref[band, where, :], height, width)
         put = split_cell(put_ref[band, where, :], height, width)
-        live = slot + at * block < count_ref[band]
+        live = slot + at * block < count_ref[0, 0, 0, band]
         return pull, put, jnp.where(live, weight_ref[band, where, :], 0.0)
 
     def blocks(band):
-        return (count_ref[band] + block - 1) // block
+        return (count_ref[0, 0, 0, band] + block - 1) // block
 
     total_ref[...] = jnp.zeros_like(total_ref)
 
@@ -350,9 +350,15 @@
     increment_ref,
     diffusivity_ref,
     land_ref,
+    pull_ref,
+    put_ref,
+    weight_ref,
     state_ref,
     fixed_ref,
     source_ref,
+    pull_lines,
+    put_lines,
+    weight_lines,
     field,
     surface,
     surfaces,
@@ -385,6 +391,11 @@
         return carry
 
     lax.fori_loop(0, levels, fill, 0)
+    for line in range(pull_lines.shape[1]):
+        lanes = pl.ds(line * LANES, LANES)
+        pull_lines[:, line, :] = pull_ref[:, lanes]
+        put_lines[:, line, :] = put_ref[:, lanes]
+        weight_lines[:, line, :] = weight_ref[:, lanes]
     for copy in lon_copies(0, lons):
         copy.wait_recv()
     for k in range(levels):
@@ -506,13 +517,6 @@
             value = stepped(value, coefficients)
         gradient_ref[k] = value[:height, :width] + increment_ref[k]
 
-    for copy in lon_copies(1, lons):
-        copy.wait_recv()
-    field[(0,) + side] = lon_unpack(lon_came, 1, 0)
-    wide = field[0, rows, :]
-    lat_pack(lat_sent_ref, 0, wide, wide)
-    lat_start(0, lats)
-
     def couple_of(pair, carry):
         later = jnp.minimum(2 * pair, levels - 1)
         upper, lower = lat_came(pair, lats)
@@ -522,7 +526,14 @@
         pl.when(2 * pair < levels)(lambda: sweep(later))
         return carry
 
-    lax.fori_loop(1, pairs + 1, couple_of, 0)
+    lax.fori_loop(1, pairs // 2 + 1, couple_of, 0)
+    for copy in lon_copies(1, lons):
+        copy.wait_recv()
+    field[(0,) + side] = lon_unpack(lon_came, 1, 0)
+    wide = field[0, rows, :]
+    lat_pack(lat_sent_ref, 0, wide, wide)
+    lat_start(0, lats)
+    lax.fori_loop(pairs // 2 + 1, pairs + 1, couple_of, 0)
     field[0, ends, :] = lat_came(0, lats)[0]
     sweep(0)
     for at in range(2):
@@ -567,17 +578,26 @@
         ]
 
     block = real(levels, height, width)
-    state, fixed, source = pl.pallas_call(
+    slots = jax.ShapeDtypeStruct((bands, lines, LANES), jnp.int32)
+    state, fixed, source, pull, put, weight = pl.pallas_call(
         forward_kernel,
-        out_shape=(block, real(levels + 1, tall, wide), real(bands, rows, LANES)),
-        in_specs=[whole] * 3,
-        out_specs=(whole,) * 3,
+        out_shape=(block, real(levels + 1, tall, wide), real(bands, rows, LANES))
+        + (slots, slots, real(bands, lines, LANES)),
+        in_specs=[whole] * 6,
+        out_specs=(whole,) * 6,
         scratch_shapes=[room(levels, tall, wide), room(rows, LANES), room(bands, rows, LANES)]
         + halos(1, levels + 1),
         compiler_params=pltpu.CompilerParams(
             vmem_limit_bytes=space, collective_id=0, has_side_effects=True
         ),
-    )(increment[0], diffusivity[0], land_mask)
+    )(
+        increment[0],
+        diffusivity[0],
+        land_mask,
+        pull_cells.reshape(bands, -1),
+        put_cells.reshape(bands, -1),
+        pull_weight.reshape(bands, -1),
+    )
 
     linear, adjoint, sums = pl.pallas_call(
         functools.partial(couple_kernel, height, width),
@@ -587,11 +607,11 @@
         scratch_shapes=[room(2 * rows, LANES), room(rows, LANES)],
         compiler_params=pltpu.CompilerParams(vmem_limit_bytes=space),
     )(
-        pull_count.reshape(bands),
+        pull_count,
         source,
-        pull_cells.reshape(bands, lines, LANES),
-        put_cells.reshape(bands, lines, LANES),
-        pull_weight.reshape(bands, lines, LANES),
+        pull,
+        put,
+        weight,
         land_mask,
         state,
         innovation[0],

time: 46.3 us -> 49.8 us (1.076)
  local copies, waits for them, and re-layouts: 3.37 us -> 6.72 us
    unnamed x14 -> x19, local copies, waits for them, and re-layouts: 2.39 us -> 6.72 us
    reshape x1 -> x0, local copies, waits for them, and re-layouts: 0.98 us -> none  [local(): put_cells.reshape(bands, lines, LANES)]
where the time goes in v4:
time: 49.8 us; the launch traced here: 49.5 us
  Pallas kernels  42.1 us (85%)
  local copies, waits for them, and re-layouts  6.72 us (13%)
  between operations  0.68 us (1%)
    pallas_call x1, Pallas kernels, local(): pl.pallas_call(forward_kernel, out_shape=(block, real(levels + 1, tall, w...  16.7 us
    pallas_call x1, Pallas kernels, local(): pl.pallas_call(adjoint_kernel, out_shape=block, in_specs=[whole] * 4, out...  14.6 us
    pallas_call x1, Pallas kernels, local(): pl.pallas_call(functools.partial(couple_kernel, height, width), out_shape...  10.8 us
    unnamed x19, local copies, waits for them, and re-layouts  6.72 us

profile of v4, /device:TPU:0, one launch (start us, length us, event | category | flops | bytes accessed | tf_op | source)
XLA Modules:
  0.0 49.5 jit_solution(3603006667249367983)
XLA Ops:
  0.6 0.0 copy-start
  0.6 0.9 %copy-done = f32[1,8,16,512]{3,2,1,0:T(8,128)S(1)} copy-done((f32[1,8,16,512]{3,2,1,0:T(8,128)S(1)}, f32[1,8,16,512]{3,2,1,0:T(8,128)}, u32[]{:S(2)}) %copy-start) | copy-done | bytes 262168
  1.6 0.0 copy-start.2
  1.6 0.9 %copy-done.2 = f32[1,8,16,512]{3,2,1,0:T(8,128)S(1)} copy-done((f32[1,8,16,512]{3,2,1,0:T(8,128)S(1)}, f32[1,8,16,512]{3,2,1,0:T(8,128)}, u32[]{:S(2)}) %copy-start.2) | copy-done | bytes 262168
  2.5 0.0 copy-start.4
  2.5 0.9 %copy-done.4 = s32[1,1,1,4,8192]{4,3,2,1,0:T(4,128)S(1)} copy-done((s32[1,1,1,4,8192]{4,3,2,1,0:T(4,128)S(1)}, s32[1,1,1,4,8192]{4,3,2,1,0:T(4,128)}, u32[]{:S(2)}) %copy-start.4) | copy-done | bytes 131096
  3.4 0.0 copy-start.5
  3.4 0.9 %copy-done.5 = s32[1,1,1,4,8192]{4,3,2,1,0:T(4,128)S(1)} copy-done((s32[1,1,1,4,8192]{4,3,2,1,0:T(4,128)S(1)}, s32[1,1,1,4,8192]{4,3,2,1,0:T(4,128)}, u32[]{:S(2)}) %copy-start.5) | copy-done | bytes 131096
  4.3 0.0 copy-start.6
  4.3 0.9 %copy-done.6 = f32[1,1,1,4,8192]{4,3,2,1,0:T(4,128)S(1)} copy-done((f32[1,1,1,4,8192]{4,3,2,1,0:T(4,128)S(1)}, f32[1,1,1,4,8192]{4,3,2,1,0:T(4,128)}, u32[]{:S(2)}) %copy-start.6) | copy-done | bytes 131096
  5.2 0.0 copy-start.7
  5.3 0.8 %copy-done.7 = s32[16,512]{1,0:T(8,128)S(1)} copy-done((s32[16,512]{1,0:T(8,128)S(1)}, s32[16,512]{1,0:T(8,128)}, u32[]{:S(2)}) %copy-start.7) | copy-done | bytes 32792
  6.0 0.0 copy-start.3
  6.0 16.7 %shard_map.95 = (f32[8,16,512]{2,1,0:T(8,128)S(1)}, f32[9,24,640]{2,1,0:T(8,128)S(1)}, f32[4,64,128]{2,1,0:T(8,128)S(1)}, s32[4,64,128]{2,1,0:T(8,128)S(1)}, s32...) custom-call(f32[8,16,512]{2,1,0:T(8,128)S(1)} %bitcast.9, f32[8,16,512]{2,1,0:T(8,128)S(1)} %bitcast.11, ...), custom_call_target="tpu_custom_call" | custom-call | tf_op jit(solution)/shard_map/pallas_call | solution.py:582
  22.7 0.0 copy-start.8
  22.7 0.0 copy-done.3
  22.7 0.6 %copy-done.8 = s32[1,1,1,4]{3,2,1,0:T(1,128)S(1)} copy-done((s32[1,1,1,4]{3,2,1,0:T(1,128)S(1)}, s32[1,1,1,4]{3,2,1,0:T(1,128)}, u32[]{:S(2)}) %copy-start.8) | copy-done | bytes 40
  23.3 0.0 copy-start.1
  23.3 10.8 %shard_map.96 = (f32[8,16,512]{2,1,0:T(8,128)}, f32[8,16,512]{2,1,0:T(8,128)S(1)}, f32[4,64,128]{2,1,0:T(8,128)S(1)}) custom-call(s32[1,1,1,4]{3,2,1,0:T(1,128)S(1)} %copy-done.8, f32[4,64,128]{2,1,0:T(8,128)S(1)} %get-tuple-element.11.source_ref, s32[4,64,128]{2,1,0:T(8,128)S(1)} %get-tuple-element.12.pull_ref, ...), custom_call_target="tpu_custom_call" | custom-call | tf_op jit(solution)/shard_map/pallas_call | solution.py:602
  34.1 0.0 copy-done.1
  34.1 14.6 %shard_map.97 = f32[8,16,512]{2,1,0:T(8,128)S(1)} custom-call(f32[8,16,512]{2,1,0:T(8,128)S(1)} %get-tuple-element.17.adjoint_ref, f32[4,64,128]{2,1,0:T(8,128)S(1)} %get-tuple-element.18.sums_ref, f32[9,24,640]{2,1,0:T(8,128)S(1)} %get-tuple-element.19.fixed_ref, f32[8,16,512]{2,1,0:T(8,128)S(1)} %bitcast.10), custom_call_target="tpu_custom_call" | custom-call | tf_op jit(solution)/shard_map/pallas_call | solution.py:620
  48.8 0.7 %copy.11 = f32[1,8,16,512]{3,2,1,0:T(8,128)} copy(f32[1,8,16,512]{3,2,1,0:T(8,128)S(1)} %bitcast.8) | data formatting | bytes 524288
Async XLA Ops:
  0.6 1.0 %copy-start = (f32[1,8,16,512]{3,2,1,0:T(8,128)S(1)}, f32[1,8,16,512]{3,2,1,0:T(8,128)}, u32[]{:S(2)}) copy-start(f32[1,8,16,512]{3,2,1,0:T(8,128)} %param.8) | copy-start | bytes 786436
  1.6 0.9 %copy-start.2 = (f32[1,8,16,512]{3,2,1,0:T(8,128)S(1)}, f32[1,8,16,512]{3,2,1,0:T(8,128)}, u32[]{:S(2)}) copy-start(f32[1,8,16,512]{3,2,1,0:T(8,128)} %param.9) | copy-start | bytes 786436
  2.5 0.9 %copy-start.4 = (s32[1,1,1,4,8192]{4,3,2,1,0:T(4,128)S(1)}, s32[1,1,1,4,8192]{4,3,2,1,0:T(4,128)}, u32[]{:S(2)}) copy-start(s32[1,1,1,4,8192]{4,3,2,1,0:T(4,128)} %param.12) | copy-start | bytes 393220
  3.4 0.9 %copy-start.5 = (s32[1,1,1,4,8192]{4,3,2,1,0:T(4,128)S(1)}, s32[1,1,1,4,8192]{4,3,2,1,0:T(4,128)}, u32[]{:S(2)}) copy-start(s32[1,1,1,4,8192]{4,3,2,1,0:T(4,128)} %param.13) | copy-start | bytes 393220
  4.3 0.9 %copy-start.6 = (f32[1,1,1,4,8192]{4,3,2,1,0:T(4,128)S(1)}, f32[1,1,1,4,8192]{4,3,2,1,0:T(4,128)}, u32[]{:S(2)}) copy-start(f32[1,1,1,4,8192]{4,3,2,1,0:T(4,128)} %param.14) | copy-start | bytes 393220
  5.2 0.8 %copy-start.7 = (s32[16,512]{1,0:T(8,128)S(1)}, s32[16,512]{1,0:T(8,128)}, u32[]{:S(2)}) copy-start(s32[16,512]{1,0:T(8,128)} %land_ref.3) | copy-start | bytes 98308
  6.0 16.7 %copy-start.3 = (f32[1,8,16,512]{3,2,1,0:T(8,128)S(1)}, f32[1,8,16,512]{3,2,1,0:T(8,128)}, u32[]{:S(2)}) copy-start(f32[1,8,16,512]{3,2,1,0:T(8,128)} %param.10) | copy-start | bytes 786436
  22.7 0.7 %copy-start.8 = (s32[1,1,1,4]{3,2,1,0:T(1,128)S(1)}, s32[1,1,1,4]{3,2,1,0:T(1,128)}, u32[]{:S(2)}) copy-start(s32[1,1,1,4]{3,2,1,0:T(1,128)} %count_ref.1) | copy-start | bytes 52
  23.3 10.8 %copy-start.1 = (f32[1,8,16,512]{3,2,1,0:T(8,128)S(1)}, f32[1,8,16,512]{3,2,1,0:T(8,128)}, u32[]{:S(2)}) copy-start(f32[1,8,16,512]{3,2,1,0:T(8,128)} %param.8) | copy-start | bytes 786436

commit v5 on v4

--- a/solution.py
+++ b/solution.py
@@ -347,18 +347,25 @@
 
 
 def forward_kernel(
+    increment_far,
+    diffusivity_far,
+    land_far,
+    pull_far,
+    put_far,
+    weight_far,
+    state_ref,
+    fixed_ref,
+    source_ref,
+    pull_lines,
+    put_lines,
+    weight_lines,
     increment_ref,
     diffusivity_ref,
     land_ref,
     pull_ref,
     put_ref,
     weight_ref,
-    state_ref,
-    fixed_ref,
-    source_ref,
-    pull_lines,
-    put_lines,
-    weight_lines,
+    load_sems,
     field,
     surface,
     surfaces,
@@ -371,7 +378,24 @@
     band_sems,
 ):
     levels, height, width = increment_ref.shape
+    loads = [
+        pltpu.make_async_copy(far, near, load_sems.at[at])
+        for at, (far, near) in enumerate(
+            (
+                (increment_far, increment_ref),
+                (diffusivity_far, diffusivity_ref),
+                (land_far, land_ref),
+                (pull_far, pull_ref),
+                (put_far, put_ref),
+                (weight_far, weight_ref),
+            )
+        )
+    ]
+    for load in loads:
+        load.start()
     greet(*edges())
+    for load in loads[:3]:
+        load.wait()
     ocean = lax.axis_index("comp") == 1
     mask = jnp.where(ocean, land_ref[...].astype(jnp.float32), 1.0)
     lons = (lon_sent, lon_came, lon_sems)
@@ -391,6 +415,8 @@
         return carry
 
     lax.fori_loop(0, levels, fill, 0)
+    for load in loads[3:]:
+        load.wait()
     for line in range(pull_lines.shape[1]):
         lanes = pl.ds(line * LANES, LANES)
         pull_lines[:, line, :] = pull_ref[:, lanes]
@@ -558,7 +584,7 @@
     tall, wide = height + 2 * HALO, width + LANES
     pairs = levels // 2
     whole = pl.BlockSpec(memory_space=pltpu.VMEM)
-    space = 48 * 1024 * 1024
+    space = 62 * 1024 * 1024
 
     def real(*shape):
         return jax.ShapeDtypeStruct(shape, jnp.float32)
@@ -583,9 +609,18 @@
         forward_kernel,
         out_shape=(block, real(levels + 1, tall, wide), real(bands, rows, LANES))
         + (slots, slots, real(bands, lines, LANES)),
-        in_specs=[whole] * 6,
+        in_specs=[pl.BlockSpec(memory_space=pltpu.HBM)] * 6,
         out_specs=(whole,) * 6,
-        scratch_shapes=[room(levels, tall, wide), room(rows, LANES), room(bands, rows, LANES)]
+        scratch_shapes=[
+            room(levels, height, width),
+            room(levels, height, width),
+            pltpu.VMEM((height, width), jnp.int32),
+            pltpu.VMEM((bands, lines * LANES), jnp.int32),
+            pltpu.VMEM((bands, lines * LANES), jnp.int32),
+            room(bands, lines * LANES),
+            pltpu.SemaphoreType.DMA((6,)),
+        ]
+        + [room(levels, tall, wide), room(rows, LANES), room(bands, rows, LANES)]
         + halos(1, levels + 1),
         compiler_params=pltpu.CompilerParams(
             vmem_limit_bytes=space, collective_id=0, has_side_effects=True

time: 49.8 us -> 48.8 us (0.980)
  local copies, waits for them, and re-layouts: 6.72 us -> 1.67 us
  Pallas kernels: 42.1 us -> 46.3 us
    unnamed x19 -> x1, local copies, waits for them, and re-layouts: 6.72 us -> 1.67 us
    pallas_call x1, Pallas kernels: 14.6 us -> 16.7 us  [local(): pl.pallas_call(adjoint_kernel, out_shape=block, in_specs=[whole] * 4, out...]
    pallas_call x1, Pallas kernels: 16.7 us -> 17.9 us  [local(): pl.pallas_call(forward_kernel, out_shape=(block, real(levels + 1, tall, w...]
    pallas_call x1, Pallas kernels: 10.8 us -> 11.7 us  [local(): pl.pallas_call(functools.partial(couple_kernel, height, width), out_shape...]
where the time goes in v5:
time: 48.8 us; the launch traced here: 48.6 us
  Pallas kernels  46.3 us (95%)
  local copies, waits for them, and re-layouts  1.67 us (3%)
  between operations  0.65 us (1%)
    pallas_call x1, Pallas kernels, local(): pl.pallas_call(forward_kernel, out_shape=(block, real(levels + 1, tall, w...  17.9 us
    pallas_call x1, Pallas kernels, local(): pl.pallas_call(adjoint_kernel, out_shape=block, in_specs=[whole] * 4, out...  16.7 us
    pallas_call x1, Pallas kernels, local(): pl.pallas_call(functools.partial(couple_kernel, height, width), out_shape...  11.7 us
    unnamed x1, local copies, waits for them, and re-layouts  1.67 us

profile of v5, /device:TPU:0, one launch (start us, length us, event | category | flops | bytes accessed | tf_op | source)
XLA Modules:
  0.0 48.6 jit_solution(13833547464733439566)
XLA Ops:
  0.6 17.9 %shard_map.95 = (f32[8,16,512]{2,1,0:T(8,128)}, f32[9,24,640]{2,1,0:T(8,128)}, f32[4,64,128]{2,1,0:T(8,128)}, s32[4,64,128]{2,1,0:T(8,128)}, s32[4,64,128]{2,1,0:T(8,128)}, /*index=5*/f32[4,64,128]{2,1,0:T(8,128)}) custom-call(f32[8,16,512]{2,1,0:T(8,128)} %bitcast.9, f32[8,16,512]{2,1,0:T(8,128)} %bitcast.11, s32[16,512]{1,0:T(8,128)} %land_ref.1, ...), custom_call_target="tpu_custom_call" | custom-call | tf_op jit(solution)/shard_map/pallas_call | solution.py:608
  18.5 11.7 %shard_map.96 = (f32[8,16,512]{2,1,0:T(8,128)}, f32[8,16,512]{2,1,0:T(8,128)}, f32[4,64,128]{2,1,0:T(8,128)}) custom-call(s32[1,1,1,4]{3,2,1,0:T(1,128)} %count_ref.1, f32[4,64,128]{2,1,0:T(8,128)} %get-tuple-element.11.source_ref, s32[4,64,128]{2,1,0:T(8,128)} %get-tuple-element.12.pull_ref, s32[4,64,128]{2,1,0:T(8,128)} %get-tuple-element.13.put_ref, ...), custom_call_target="tpu_custom_call" | custom-call | tf_op jit(solution)/shard_map/pallas_call | solution.py:637
  30.2 16.7 %shard_map.97 = f32[8,16,512]{2,1,0:T(8,128)} custom-call(f32[8,16,512]{2,1,0:T(8,128)} %get-tuple-element.17.adjoint_ref, f32[4,64,128]{2,1,0:T(8,128)} %get-tuple-element.18.sums_ref, f32[9,24,640]{2,1,0:T(8,128)} %get-tuple-element.19.fixed_ref, f32[8,16,512]{2,1,0:T(8,128)} %bitcast.10), custom_call_target="tpu_custom_call" | custom-call | tf_op jit(solution)/shard_map/pallas_call | solution.py:655
  46.9 1.7 %copy.11 = f32[1,8,16,512]{3,2,1,0:T(8,128)} copy(f32[1,8,16,512]{3,2,1,0:T(8,128)} %bitcast.8) | data formatting | bytes 524288

commit v6 on v3

--- a/solution.py
+++ b/solution.py
@@ -506,13 +506,6 @@
             value = stepped(value, coefficients)
         gradient_ref[k] = value[:height, :width] + increment_ref[k]
 
-    for copy in lon_copies(1, lons):
-        copy.wait_recv()
-    field[(0,) + side] = lon_unpack(lon_came, 1, 0)
-    wide = field[0, rows, :]
-    lat_pack(lat_sent_ref, 0, wide, wide)
-    lat_start(0, lats)
-
     def couple_of(pair, carry):
         later = jnp.minimum(2 * pair, levels - 1)
         upper, lower = lat_came(pair, lats)
@@ -522,7 +515,14 @@
         pl.when(2 * pair < levels)(lambda: sweep(later))
         return carry
 
-    lax.fori_loop(1, pairs + 1, couple_of, 0)
+    lax.fori_loop(1, pairs // 2 + 1, couple_of, 0)
+    for copy in lon_copies(1, lons):
+        copy.wait_recv()
+    field[(0,) + side] = lon_unpack(lon_came, 1, 0)
+    wide = field[0, rows, :]
+    lat_pack(lat_sent_ref, 0, wide, wide)
+    lat_start(0, lats)
+    lax.fori_loop(pairs // 2 + 1, pairs + 1, couple_of, 0)
     field[0, ends, :] = lat_came(0, lats)[0]
     sweep(0)
     for at in range(2):

time: 46.3 us -> 46.4 us (level)
  no operation moved by 1% of the time
where the time goes in v6:
time: 46.4 us; the launch traced here: 46.2 us
  Pallas kernels  42.1 us (91%)
  local copies, waits for them, and re-layouts  3.37 us (7%)
  between operations  0.73 us (2%)
    pallas_call x1, Pallas kernels, local(): pl.pallas_call(forward_kernel, out_shape=(block, real(levels + 1, tall, w...  16.7 us
    pallas_call x1, Pallas kernels, local(): pl.pallas_call(adjoint_kernel, out_shape=block, in_specs=[whole] * 4, out...  14.6 us
    pallas_call x1, Pallas kernels, local(): pl.pallas_call(functools.partial(couple_kernel, height, width), out_shape...  10.8 us
    unnamed x14, local copies, waits for them, and re-layouts  2.39 us
    reshape x1, local copies, waits for them, and re-layouts, local(): put_cells.reshape(bands, lines, LANES)  0.98 us

profile of v6, /device:TPU:0, one launch (start us, length us, event | category | flops | bytes accessed | tf_op | source)
XLA Modules:
  0.0 46.2 jit_solution(4400125037038362110)
XLA Ops:
  0.6 0.0 copy-start.5
  0.6 0.0 copy-start.3
  0.7 0.9 %copy.16 = f32[1,4,64,128]{3,2,1,0:T(8,128)S(1)} copy(f32[1,4,64,128]{3,1,2,0:T(4,128)} %bitcast.26) | data formatting | bytes 262144
  1.6 0.0 copy-done.5
  1.6 0.0 copy-start
  1.6 0.0 copy-start.1
  1.6 1.0 %copy_bitcast_fusion.1 = (s32[4,64,128]{2,1,0:T(8,128)S(1)}, s32[4,64,128]{2,1,0:T(8,128)S(1)}) fusion(s32[1,4,64,128]{3,1,2,0:T(4,128)S(1)} %bitcast.27, s32[1,4,64,128]{3,1,2,0:T(4,128)} %bitcast.28), kind=kLoop, calls=%fused_computation.1 | loop fusion | bytes 524288 | tf_op jit(solution)/shard_map/reshape | solution.py:593
  2.6 0.0 copy-done.3
  2.6 0.0 copy-done
  2.6 0.1 copy-done.1
  2.7 0.0 copy-start.2
  2.7 16.7 %shard_map.95 = (f32[8,16,512]{2,1,0:T(8,128)S(1)}, f32[9,24,640]{2,1,0:T(8,128)S(1)}, f32[4,64,128]{2,1,0:T(8,128)S(1)}) custom-call(f32[8,16,512]{2,1,0:T(8,128)S(1)} %bitcast.19, f32[8,16,512]{2,1,0:T(8,128)S(1)} %bitcast.23, s32[16,512]{1,0:T(8,128)S(1)} %copy-done.3), custom_call_target="tpu_custom_call" | custom-call | tf_op jit(solution)/shard_map/pallas_call | solution.py:570
  19.4 0.0 copy-start.4
  19.4 0.0 copy-done.2
  19.4 0.6 %copy-done.4 = s32[1,1,1,4]{3,2,1,0:T(1,128)S(1)} copy-done((s32[1,1,1,4]{3,2,1,0:T(1,128)S(1)}, s32[1,1,1,4]{3,2,1,0:T(1,128)}, u32[]{:S(2)}) %copy-start.4) | copy-done | bytes 40
  20.1 10.8 %shard_map.96 = (f32[8,16,512]{2,1,0:T(8,128)}, f32[8,16,512]{2,1,0:T(8,128)S(1)}, f32[4,64,128]{2,1,0:T(8,128)S(1)}) custom-call(s32[4]{0:T(128)S(1)} %bitcast.25, f32[4,64,128]{2,1,0:T(8,128)S(1)} %get-tuple-element.8.source_ref, s32[4,64,128]{2,1,0:T(8,128)S(1)} %get-tuple-element.15.pull_ref, s32[4,64,128]{2,1,0:T(8,128)S(1)} %get-tuple-element.14.put_ref, ...), custom_call_target="tpu_custom_call" | custom-call | tf_op jit(solution)/shard_map/pallas_call | solution.py:582
  30.9 14.6 %shard_map.97 = f32[8,16,512]{2,1,0:T(8,128)S(1)} custom-call(f32[8,16,512]{2,1,0:T(8,128)S(1)} %get-tuple-element.11.adjoint_ref, f32[4,64,128]{2,1,0:T(8,128)S(1)} %get-tuple-element.12.sums_ref, f32[9,24,640]{2,1,0:T(8,128)S(1)} %get-tuple-element.13.fixed_ref, f32[8,16,512]{2,1,0:T(8,128)S(1)} %bitcast.20), custom_call_target="tpu_custom_call" | custom-call | tf_op jit(solution)/shard_map/pallas_call | solution.py:600
  45.5 0.7 %copy.18 = f32[1,8,16,512]{3,2,1,0:T(8,128)} copy(f32[1,8,16,512]{3,2,1,0:T(8,128)S(1)} %bitcast.21) | data formatting | bytes 524288
Async XLA Ops:
  0.6 1.0 %copy-start.5 = (s32[1,1,1,4,8192]{4,3,2,1,0:T(4,128)S(1)}, s32[1,1,1,4,8192]{4,3,2,1,0:T(4,128)}, u32[]{:S(2)}) copy-start(s32[1,1,1,4,8192]{4,3,2,1,0:T(4,128)} %param.13) | copy-start | bytes 393220
  0.6 2.0 %copy-start.3 = (s32[16,512]{1,0:T(8,128)S(1)}, s32[16,512]{1,0:T(8,128)}, u32[]{:S(2)}) copy-start(s32[16,512]{1,0:T(8,128)} %land_ref.3) | copy-start | bytes 98308
  1.6 1.0 %copy-start = (f32[1,8,16,512]{3,2,1,0:T(8,128)S(1)}, f32[1,8,16,512]{3,2,1,0:T(8,128)}, u32[]{:S(2)}) copy-start(f32[1,8,16,512]{3,2,1,0:T(8,128)} %param.8) | copy-start | bytes 786436
  1.6 1.1 %copy-start.1 = (f32[1,8,16,512]{3,2,1,0:T(8,128)S(1)}, f32[1,8,16,512]{3,2,1,0:T(8,128)}, u32[]{:S(2)}) copy-start(f32[1,8,16,512]{3,2,1,0:T(8,128)} %param.9) | copy-start | bytes 786436
  2.7 16.7 %copy-start.2 = (f32[1,8,16,512]{3,2,1,0:T(8,128)S(1)}, f32[1,8,16,512]{3,2,1,0:T(8,128)}, u32[]{:S(2)}) copy-start(f32[1,8,16,512]{3,2,1,0:T(8,128)} %param.10) | copy-start | bytes 786436
  19.4 0.7 %copy-start.4 = (s32[1,1,1,4]{3,2,1,0:T(1,128)S(1)}, s32[1,1,1,4]{3,2,1,0:T(1,128)}, u32[]{:S(2)}) copy-start(s32[1,1,1,4]{3,2,1,0:T(1,128)} %param.15) | copy-start | bytes 52
